TPU v7x, 128 devices: a whole 4x4x4 slice. The times are simulated.
128 devices in a mesh: ctx: 16 (over x, y_lo, core), enc: 8 (over z, y_hi).
Axes of the slice: x: 4, y: 4 (y_hi: 2, y_lo: 2; y = y_hi * 2 + y_lo), z: 4, core: 2. Of those that a mesh axis runs over, the one named last changes fastest.
Arguments:
- self_q: bfloat16 [4096, 4096], P('ctx', 'enc')
- self_k: bfloat16 [4096, 4096], P('ctx', 'enc')
- self_v: bfloat16 [4096, 4096], P('ctx', 'enc'), may hold values from -6 to 6
- cross_q: bfloat16 [4096, 4096], P('ctx', 'enc'), may hold values from -6 to 6
- cross_k_weight: bfloat16 [896, 4096], P(None, 'enc'), may hold values from -0.1875 to 0.1875
- cross_v_weight: bfloat16 [896, 4096], P(None, 'enc'), may hold values from -0.1875 to 0.1875
- span_ctx: bfloat16 [4096, 896], P('ctx'), may hold values from -6 to 6
- neighbours: bfloat16 [256, 128, 896], P(('ctx', 'enc')), may hold values from -6 to 6
- neighbour_ids: int32 [64, 2], P('ctx'), may hold values from 0 to 15, as said below
- enc_q: bfloat16 [896, 896], replicated, may hold values from -0.1875 to 0.1875
- enc_k: bfloat16 [896, 896], replicated, may hold values from -0.1875 to 0.1875
- enc_v: bfloat16 [896, 896], replicated, may hold values from -0.1875 to 0.1875
- enc_o: bfloat16 [896, 896], replicated, may hold values from -0.1875 to 0.1875
- mixed_grad: bfloat16 [4096, 4096], P('ctx', 'enc'), may hold values from -6 to 6
Outputs:
- mixed: bfloat16 [4096, 4096], P('ctx', 'enc')
- neighbour_grad: float32 [256, 128, 896], P(('ctx', 'enc'))
Inputs may be any that keep to these rules, and one draw needn't show every extreme that they name: `neighbour_ids`: within the 4 spans of one ctx index the 8 values are distinct slots; slot g of that index is held by enc index g // 2; in every such group some enc index has all of its 2 slots named.
All inputs are finite; a program needn't handle non-finite values.
Results may differ from a plain program's by a relative error of at most 0.025.
Values may be sent and summed in bfloat16 or wider, within the bound.
No kernel may reach another device: no remote copies, remote signals or barrier semaphores. Data moves between devices by JAX's collectives and lax.ppermute only.
A program may use at most 128 MiB of HBM per device.

v0:
```python
import math

import jax
import jax.numpy as jnp
from jax import lax
from jax.experimental import pallas as pl
from jax.experimental.pallas import tpu as pltpu
from jax.sharding import Mesh
from jax.sharding import PartitionSpec as P

HSIZE = 128
EHEADS = 4
CL = 64
NL = 128
NX = 4
LOG2E = math.log2(math.e)
BF16 = jnp.bfloat16
F32 = jnp.float32

NT = (((1,), (1,)), ((), ()))
TN = (((0,), (0,)), ((), ()))


def mm(a, b):
    return jnp.dot(a, b, preferred_element_type=F32)


def mm_nt(a, b):
    return lax.dot_general(a, b, NT, preferred_element_type=F32)


def mm_tn(a, b):
    return lax.dot_general(a, b, TN, preferred_element_type=F32)


def call(kernel, mib=24, **kw):
    return pl.pallas_call(
        kernel,
        compiler_params=pltpu.CompilerParams(vmem_limit_bytes=mib * 1024 * 1024),
        **kw,
    )


def smem():
    return pl.BlockSpec(memory_space=pltpu.SMEM)


def vmem():
    return pl.BlockSpec(memory_space=pltpu.VMEM)


def hbm():
    return pl.BlockSpec(memory_space=pltpu.HBM)


def pack_kernel(q_ref, k_ref, v_ref, out):
    for h in range(NX):
        cols = slice(h * HSIZE, (h + 1) * HSIZE)
        for i, src in enumerate((q_ref, k_ref, v_ref)):
            out[h, i] = src[:, cols]


def attend_kernel(pieces, kv0, kv1, kv2, kv3, o0, o1, o2, o3, acc, top):
    kv = (kv0, kv1, kv2, kv3)
    x = lax.axis_index("x")
    r = lax.axis_index("yl") * 2 + lax.axis_index("core")
    scale = LOG2E / math.sqrt(HSIZE)
    rows = pieces.shape[2]
    ones = jnp.ones((rows, HSIZE), BF16)
    for xq in range(NX):
        q = pieces[xq, 0]

        def group(xk):
            scores = [mm_nt(q, kv[i][xk, 0]) for i in range(4)]
            if xk == xq:
                at = lax.broadcasted_iota(jnp.int32, (rows, rows), 1)
                upto = lax.broadcasted_iota(jnp.int32, (rows, rows), 0)
                scores = [
                    jnp.where(at + jnp.bitwise_xor(r, i) * rows <= upto + r * rows, s, -1e30)
                    for i, s in enumerate(scores)
                ]
            best = jnp.maximum(
                jnp.maximum(scores[0], scores[1]), jnp.maximum(scores[2], scores[3])
            )
            new = jnp.max(best, axis=-1, keepdims=True)
            if xk > 0:
                old = top[...]
                new = jnp.maximum(old, new)
            out = None
            for i, s in enumerate(scores):
                weights = jnp.exp2((s - new) * scale).astype(BF16)
                term = mm(weights, jnp.concatenate([kv[i][xk, 1], ones], axis=1))
                out = term if out is None else out + term
            if xk > 0:
                out = acc[...] * jnp.exp2((old - new) * scale) + out
            acc[...] = out
            top[...] = new

        for xk in range(xq + 1):
            group(xk)
        total = acc[...]
        result = (total[:, :HSIZE] / total[:, HSIZE:]).astype(BF16)
        for d, out in enumerate((o0, o1, o2, o3)):

            @pl.when(lax.rem(xq + d, NX) == x)
            def _():
                out[...] = result


def mix_kernel(s0, s1, s2, s3, cross, out):
    x = lax.axis_index("x")
    for d, piece in enumerate((s0, s1, s2, s3)):
        cols = pl.ds(pl.multiple_of(lax.rem(x + d, NX) * HSIZE, HSIZE), HSIZE)
        out[:, cols] = (piece[...].astype(F32) + cross[:, cols]).astype(BF16)


def head_rows(rows):
    width = rows.shape[1]
    each = width // EHEADS
    at = lax.broadcasted_iota(jnp.int32, (1, width), 1)
    parts = []
    for h in range(EHEADS):
        keep = jnp.where((at >= h * each) & (at < (h + 1) * each), 1.0, 0.0).astype(BF16)
        parts.append(rows * keep)
    return jnp.concatenate(parts, axis=0)


def encode_kernel(
    ids, nb_h, ctx_h, wq_h, wk_h, wv_h, wo_h, enc, wt, ek_out, ev_out, *scratch
):
    nb, ctx, wq, wk, wv, wo, sems = scratch
    both = ((nb_h, nb), (wq_h, wq), (ctx_h, ctx), (wk_h, wk), (wv_h, wv), (wo_h, wo))
    copies = [pltpu.make_async_copy(a, b, sems.at[i]) for i, (a, b) in enumerate(both)]
    for c in copies:
        c.start()
    slots, rows, width = nb.shape
    each = width // EHEADS
    copies[0].wait()
    x = nb[...].reshape(slots * rows, width)
    copies[1].wait()
    eq = mm(x, wq[...]).astype(BF16)
    copies[2].wait()
    contexts = []
    for t in range(slots):
        mine = (lax.axis_index("z") * 2 + lax.axis_index("yh")) * slots + t
        span = jnp.int32(0)
        for c in range(1, ids.shape[1]):
            span = jnp.where((ids[0, c] == mine) | (ids[1, c] == mine), c, span)
        contexts.append(ctx[pl.ds(pl.multiple_of(span * CL, CL), CL), :])
    m = jnp.concatenate(contexts, axis=0)
    copies[3].wait()
    ek = mm(m, wk[...]).astype(BF16)
    copies[4].wait()
    ev = mm(m, wv[...]).astype(BF16)
    mixed = []
    for t in range(slots):
        ek_t = ek[t * CL : (t + 1) * CL]
        ev_t = ev[t * CL : (t + 1) * CL]
        s = mm_nt(head_rows(ek_t), eq[t * rows : (t + 1) * rows]) * (1.0 / math.sqrt(each))
        s = s.reshape(EHEADS, CL, rows)
        p = jnp.exp(s - jnp.max(s, axis=1, keepdims=True))
        w = (p * (1.0 / jnp.sum(p, axis=1, keepdims=True))).reshape(EHEADS * CL, rows)
        wt[t] = w
        ek_out[t] = ek_t
        ev_out[t] = ev_t
        mixed.append(mm_tn(w.astype(BF16), head_rows(ev_t)).astype(BF16))
    copies[5].wait()
    out = x.astype(F32) + mm(jnp.concatenate(mixed, axis=0), wo[...])
    enc[...] = out.astype(BF16).reshape(slots, rows, width)


def pullback_kernel(d0, d1, d2, d3, wo, ev, wt, ek, wq, out):
    slots, rows, width = d0.shape
    each = width // EHEADS
    d = (d0[...].astype(F32) + d1[...].astype(F32)) + (d2[...].astype(F32) + d3[...].astype(F32))
    d = d.reshape(slots * rows, width)
    de = mm(d.astype(BF16), wo[...]).astype(BF16)
    back = []
    for t in range(slots):
        w = wt[t]
        dw = mm_nt(head_rows(ev[t]), de[t * rows : (t + 1) * rows])
        dw = dw.astype(BF16).astype(F32).reshape(EHEADS, CL, rows)
        w = w.reshape(EHEADS, CL, rows)
        ds = w * (dw - jnp.sum(w * dw, axis=1, keepdims=True)) * (1.0 / math.sqrt(each))
        ds = ds.reshape(EHEADS * CL, rows).astype(BF16)
        back.append(mm_tn(ds, head_rows(ek[t])).astype(BF16))
    out[...] = (d + mm(jnp.concatenate(back, axis=0), wq[...])).reshape(slots, rows, width)


def turn_kernel(wq, wo, wq_t, wo_t):
    wq_t[...] = wq[...].T
    wo_t[...] = wo[...].T


def blocks_kernel(kw, vw, q, g, kvw, kv_t, qm_t, gm_t):
    width = kw.shape[1]
    kvw[:, :width] = kw[...]
    kvw[:, width:] = vw[...]
    kv_t[:width] = kw[...].T
    kv_t[width:] = vw[...].T
    for c in range(qm_t.shape[0]):
        qm_t[c] = head_blocks(q[c * CL : (c + 1) * CL]).T
        gm_t[c] = head_blocks(g[c * CL : (c + 1) * CL]).T


def head_blocks(rows):
    width = rows.shape[1]
    at = lax.broadcasted_iota(jnp.int32, (1, width), 1)
    parts = []
    for h in range(width // HSIZE):
        keep = jnp.where((at >= h * HSIZE) & (at < (h + 1) * HSIZE), 1.0, 0.0).astype(BF16)
        parts.append(rows * keep)
    return jnp.concatenate(parts, axis=0)


def cross_kernel(ids, e00, e01, e10, e11, e20, e21, e30, e31, *rest):
    blocks = (e00, e01, e10, e11, e20, e21, e30, e31)
    kvw, qm_t, gm_t, q, g, kv_t, cross = rest[:7]
    outs, (table, held, sent, ckv, dkv) = rest[7:15], rest[15:]
    width = q.shape[1]
    z, yh = lax.axis_index("z"), lax.axis_index("yh")
    n_named = held.shape[0]
    spans = n_named // 2
    scale = 1.0 / math.sqrt(HSIZE)

    for i in range(16):
        table[i] = jnp.int32(-1)
    for n in range(n_named):
        slot = ids[n % 2, n // 2]
        dz = lax.rem(slot // 4 - z + NX, NX)
        dy = jnp.bitwise_xor(lax.rem(slot // 2, 2), yh)
        table[dz * 4 + dy * 2 + lax.rem(slot, 2)] = jnp.int32(n)
    places = [(i, t) for i in range(8) for t in range(2)]
    for i, t in places:
        n = table[2 * i + t]

        @pl.when(n >= 0)
        def _():
            held[n] = blocks[i][t]

        @pl.when(n < 0)
        def _():
            outs[i][t] = jnp.zeros(outs[i].shape[1:], BF16)

    heads = width // HSIZE
    pair = 2 * NL
    for half in range(2):
        first = half * (n_named // 2)
        e = held[first : first + n_named // 2].reshape(n_named // 2 * NL, -1)
        ckv[first * NL : (first + n_named // 2) * NL] = mm(e, kvw[...]).astype(BF16)

    def scores(c):
        at = slice(c * pair, (c + 1) * pair)
        return mm(ckv[at, :width], qm_t[c]), mm(ckv[at, width:], gm_t[c])

    def soften(s, dp):
        p = jnp.exp2((s - jnp.max(s, axis=0, keepdims=True)) * (scale * LOG2E))
        p = p * (1.0 / jnp.sum(p, axis=0, keepdims=True))
        ds = p * ((dp - jnp.sum(p * dp, axis=0, keepdims=True)) * scale)
        return p.astype(BF16), ds.astype(BF16)

    def products(c, pb, ds):
        at = slice(c * pair, (c + 1) * pair)
        dkv[at, :width] = mm(ds, head_blocks(q[c * CL : (c + 1) * CL])).astype(BF16)
        dkv[at, width:] = mm(pb, head_blocks(g[c * CL : (c + 1) * CL])).astype(BF16)
        pt = pb.T
        for h in range(heads):
            cols = slice(h * HSIZE, (h + 1) * HSIZE)
            cross[c * CL : (c + 1) * CL, cols] = mm(
                pt[h * CL : (h + 1) * CL], ckv[at, width + h * HSIZE : width + (h + 1) * HSIZE]
            )

    def back(c):
        at = slice(c * pair, (c + 1) * pair)
        sent[2 * c : 2 * c + 2] = mm(dkv[at], kv_t[...]).astype(BF16).reshape(2, NL, -1)

    def send(low, high):
        for i, t in places:
            n = table[2 * i + t]

            @pl.when((n >= low) & (n < high))
            def _():
                outs[i][t] = sent[n]

    ahead = scores(0)
    for c in range(spans):
        now = ahead
        if c + 1 < spans:
            ahead = scores(c + 1)
        soft = soften(*now)
        if c >= 1:
            back(c - 1)
        products(c, *soft)
    send(0, n_named - 2)
    back(spans - 1)
    send(n_named - 2, n_named)


def shift(n, by):
    return [(i, (i + by) % n) for i in range(n)]


def local(
    self_q,
    self_k,
    self_v,
    cross_q,
    cross_k_weight,
    cross_v_weight,
    span_ctx,
    neighbours,
    neighbour_ids,
    enc_q,
    enc_k,
    enc_v,
    enc_o,
    mixed_grad,
):
    rows, width = self_q.shape
    slots, nl, ew = neighbours.shape
    spans, per_span = neighbour_ids.shape
    n_named = spans * per_span
    struct = jax.ShapeDtypeStruct
    after = lax.optimization_barrier

    ids = neighbour_ids.T

    e00, wt, ek, ev = call(
        encode_kernel,
        mib=56,
        out_shape=[
            struct((slots, nl, ew), BF16),
            struct((slots, EHEADS * CL, nl), F32),
            struct((slots, CL, ew), BF16),
            struct((slots, CL, ew), BF16),
        ],
        in_specs=[smem()] + [hbm()] * 6,
        out_specs=[vmem()] * 4,
        scratch_shapes=[pltpu.VMEM(neighbours.shape, BF16), pltpu.VMEM(span_ctx.shape, BF16)]
        + [pltpu.VMEM((ew, ew), BF16)] * 4
        + [pltpu.SemaphoreType.DMA((6,))],
    )(ids, neighbours, span_ctx, enc_q, enc_k, enc_v, enc_o)

    e01 = lax.ppermute(e00, "yh", shift(2, 1))
    e30 = lax.ppermute(e00, "z", shift(NX, 1))
    e10 = lax.ppermute(e00, "z", shift(NX, -1))

    self_q, self_k, self_v, _ = after((self_q, self_k, self_v, wt))
    packed = call(
        pack_kernel,
        out_shape=struct((NX, 3, rows, HSIZE), BF16),
        in_specs=[vmem()] * 3,
        out_specs=vmem(),
    )(self_q, self_k, self_v)
    pieces = lax.all_to_all(packed, "x", 0, 0)

    e01, e30, e10, packed = after((e01, e30, e10, packed))
    e11 = lax.ppermute(e01, "z", shift(NX, -1))
    e31 = lax.ppermute(e01, "z", shift(NX, 1))


    weights = after((enc_q, enc_o, e01))[:2]
    turned = call(
        turn_kernel,
        out_shape=[struct((ew, ew), BF16)] * 2,
        in_specs=[vmem()] * 2,
        out_specs=[vmem()] * 2,
    )(*weights)

    own_kv = pieces[:, 1:]
    e30, e11, e31, own_kv, *turned = after((e30, e11, e31, own_kv, *turned))
    swap = [(0, 3), (1, 2), (2, 1), (3, 0)]
    kvs = [
        own_kv,
        lax.ppermute(own_kv, "core", shift(2, 1)),
        lax.ppermute(own_kv, "yl", shift(2, 1)),
        lax.ppermute(own_kv, ("yl", "core"), swap),
    ]
    wq_t, wo_t = turned
    e20 = lax.ppermute(e30, "z", shift(NX, 1))
    e21 = lax.ppermute(e11, "z", shift(NX, -1))

    given = after((cross_k_weight, cross_v_weight, cross_q, mixed_grad, e11))[:4]
    kvw, kv_t, qm_t, gm_t = call(
        blocks_kernel,
        out_shape=[struct((ew, 2 * width), BF16), struct((2 * width, ew), BF16)]
        + [struct((spans, width, width // HSIZE * CL), BF16)] * 2,
        in_specs=[vmem()] * 4,
        out_specs=[vmem()] * 4,
    )(*given)

    cross, *p = call(
        cross_kernel,
        out_shape=[struct((rows, width), F32)] + [struct((slots, nl, ew), BF16)] * 8,
        in_specs=[smem()] + [vmem()] * 14,
        out_specs=[vmem()] * 9,
        scratch_shapes=[
            pltpu.SMEM((16,), jnp.int32),
            pltpu.VMEM((n_named, nl, ew), BF16),
            pltpu.VMEM((n_named, nl, ew), BF16),
            pltpu.VMEM((n_named * nl, 2 * width), BF16),
            pltpu.VMEM((n_named * nl, 2 * width), BF16),
        ],
    )(
        ids,
        e00,
        e01,
        e10,
        e11,
        e20,
        e21,
        e30,
        e31,
        kvw,
        qm_t,
        gm_t,
        cross_q,
        mixed_grad,
        kv_t,
    )
    p00, p01, p10, p11, p20, p21, p30, p31 = p

    def add(a, b):
        return (a.astype(F32) + b.astype(F32)).astype(BF16)

    far1 = lax.ppermute(p21, "z", shift(NX, -1))
    far0 = lax.ppermute(p20, "z", shift(NX, 1))
    *kvs, _ = after((*kvs, cross))
    outs = call(
        attend_kernel,
        out_shape=[struct((rows, HSIZE), BF16)] * NX,
        in_specs=[vmem()] * 5,
        out_specs=[vmem()] * NX,
        scratch_shapes=[
            pltpu.VMEM((rows, 2 * HSIZE), F32),
            pltpu.VMEM((rows, 1), F32),
        ],
    )(pieces, *kvs)
    far1, far0, p11, *outs = after((far1, far0, p11, *outs))
    selfs = [outs[0]] + [lax.ppermute(outs[d], "x", shift(NX, -d)) for d in range(1, NX)]
    down1 = lax.ppermute(add(p31, far1), "z", shift(NX, -1))
    up1 = lax.ppermute(p11, "z", shift(NX, 1))
    near0 = add(p10, far0)
    down1, up1, near0, p30, *selfs = after((down1, up1, near0, p30, *selfs))
    theirs = (p01.astype(F32) + up1.astype(F32) + down1.astype(F32)).astype(BF16)
    other = lax.ppermute(theirs, "yh", shift(2, 1))
    up0 = lax.ppermute(near0, "z", shift(NX, 1))
    down0 = lax.ppermute(p30, "z", shift(NX, -1))

    grad = call(
        pullback_kernel,
        out_shape=struct((slots, nl, ew), F32),
        in_specs=[vmem()] * 9,
        out_specs=vmem(),
    )(p00, up0, down0, other, wo_t, ev, wt, ek, wq_t)

    mixed = call(
        mix_kernel,
        out_shape=struct((rows, width), BF16),
        in_specs=[vmem()] * 5,
        out_specs=vmem(),
    )(*selfs, cross)
    return mixed, grad


def solution(mesh):
    fine = Mesh(mesh.devices.reshape(4, 2, 2, 4, 2), ("x", "yl", "core", "z", "yh"))
    ctx, enc = ("x", "yl", "core"), ("z", "yh")
    tokens = P(ctx, enc)
    return jax.shard_map(
        local,
        mesh=fine,
        in_specs=(
            tokens,
            tokens,
            tokens,
            tokens,
            P(None, enc),
            P(None, enc),
            P(ctx, None),
            P(ctx + enc, None, None),
            P(ctx, None),
            P(),
            P(),
            P(),
            P(),
            tokens,
        ),
        out_specs=(tokens, P(ctx + enc, None, None)),
        check_vma=False,
    )
```

profile of v0, /device:TPU:0, one launch (start us, length us, event | category | flops | bytes accessed | tf_op | source)
XLA Modules:
  0.0 103.0 jit_solution(8074654398491029563)
XLA Ops:
  0.7 6.7 %shard_map.149 = (bf16[2,128,896]{2,1,0:T(8,128)(2,1)}, f32[2,256,128]{2,1,0:T(8,128)}, bf16[2,64,896]{2,1,0:T(8,128)(2,1)}, bf16[2,64,896]{2,1,0:T(8,128)(2,1)}) custom-call(s32[2,4]{1,0:T(2,128)} %bitcast.1, bf16[2,128,896]{2,1,0:T(8,128)(2,1)} %nb_h.1, bf16[256,896]{1,0:T(8,128)(2,1)} %ctx_h.1, bf16[896,896]{1,0:T(8,128)(2,1)} %wq, ...), custom_call_target="tpu_custom_call" | custom-call | tf_op jit(solution)/shard_map/pallas_call | solution.py:328
  7.4 0.0 copy-start
  7.4 3.3 %collective-permute-start = (bf16[2,128,896]{2,1,0:T(8,128)(2,1)}, bf16[2,128,896]{2,1,0:T(8,128)(2,1)}, u32[]{:S(2)}, u32[]{:S(2)}) collective-permute-start(bf16[2,128,896]{2,1,0:T(8,128)(2,1)} %get-tuple-element.62.e00), channel_id=1, source_target_pairs={{0,1},{1,0},{2,3},{3,2},{4,5},{5,4},{6,7},{7,6},{8,9},{9,8},{10,11... | collective-permute-start | bytes 1376264 | tf_op jit(solution)/shard_map/ppermute | solution.py:344
  10.7 1.9 %collective-permute-start.1 = (bf16[2,128,896]{2,1,0:T(8,128)(2,1)}, bf16[2,128,896]{2,1,0:T(8,128)(2,1)}, u32[]{:S(2)}, u32[]{:S(2)}) collective-permute-start(bf16[2,128,896]{2,1,0:T(8,128)(2,1)} %get-tuple-element.62.e00), channel_id=1, source_target_pairs={{0,2},{2,4},{4,6},{6,0},{1,3},{3,5},{5,7},{7,1},{8,10},{10,12},{12... | collective-permute-start | bytes 1376264 | tf_op jit(solution)/shard_map/ppermute | solution.py:345
  12.7 2.1 %collective-permute-start.2 = (bf16[2,128,896]{2,1,0:T(8,128)(2,1)}, bf16[2,128,896]{2,1,0:T(8,128)(2,1)}, u32[]{:S(2)}, u32[]{:S(2)}) collective-permute-start(bf16[2,128,896]{2,1,0:T(8,128)(2,1)} %get-tuple-element.62.e00), channel_id=1, source_target_pairs={{0,6},{2,0},{4,2},{6,4},{1,7},{3,1},{5,3},{7,5},{8,14},{10,8},{12,... | collective-permute-start | bytes 1376264 | tf_op jit(solution)/shard_map/ppermute | solution.py:346
  14.8 0.0 copy-done.14
  14.8 0.0 copy-done.16
  14.8 0.1 shard_map.150
  14.9 0.0 copy-start.2
  14.9 0.9 copy-done.2
  15.8 4.3 %all-to-all-start = ((bf16[4,3,256,128]{3,2,1,0:T(8,128)(2,1)}), bf16[4,3,256,128]{3,2,1,0:T(8,128)(2,1)}, u32[]{:S(2)}, u32[]{:S(2)}) async-start(bf16[4,3,256,128]{3,2,1,0:T(8,128)(2,1)} %copy-done.2), calls=%async_computation | async-start | bytes 1572864 | tf_op jit(solution)/shard_map/all_to_all | solution.py:355
  20.1 1.5 %collective-permute-done.e01 = bf16[2,128,896]{2,1,0:T(8,128)(2,1)} collective-permute-done((bf16[2,128,896]{2,1,0:T(8,128)(2,1)}, bf16[2,128,896]{2,1,0:T(8,128)(2,1)}, u32[]{:S(2)}, u32[]{:S(2)}) %collective-permute-start) | collective-permute-done | bytes 458784 | tf_op jit(solution)/shard_map/ppermute | solution.py:344
  21.6 3.8 %collective-permute-done.1.e30 = bf16[2,128,896]{2,1,0:T(8,128)(2,1)} collective-permute-done((bf16[2,128,896]{2,1,0:T(8,128)(2,1)}, bf16[2,128,896]{2,1,0:T(8,128)(2,1)}, u32[]{:S(2)}, u32[]{:S(2)}) %collective-permute-start.1) | collective-permute-done | bytes 458784 | tf_op jit(solution)/shard_map/ppermute | solution.py:345
  25.4 0.0 collective-permute-done.2.e10
  25.4 2.9 %collective-permute-start.3 = (bf16[2,128,896]{2,1,0:T(8,128)(2,1)}, bf16[2,128,896]{2,1,0:T(8,128)(2,1)}, u32[]{:S(2)}, u32[]{:S(2)}) collective-permute-start(bf16[2,128,896]{2,1,0:T(8,128)(2,1)} %collective-permute-done.e01), channel_id=1, source_target_pairs={{0,6},{2,0},{4,2},{6,4},{1,7},{3,1},{5,3},{7,5},{8,14},{10,8},{12,... | collective-permute-start | bytes 1376264 | tf_op jit(solution)/shard_map/ppermute | solution.py:358
  28.3 0.0 collective-permute-start.4
  28.3 0.9 shard_map.151
  29.2 1.2 %copy-done.3 = bf16[896,896]{1,0:T(8,128)(2,1)} copy-done((bf16[896,896]{1,0:T(8,128)(2,1)}, bf16[896,896]{1,0:T(8,128)(2,1)S(1)}, u32[]{:S(2)}) %copy-start.3) | copy-done | bytes 1605656
  30.4 1.2 %copy-done.5 = bf16[896,896]{1,0:T(8,128)(2,1)} copy-done((bf16[896,896]{1,0:T(8,128)(2,1)}, bf16[896,896]{1,0:T(8,128)(2,1)S(1)}, u32[]{:S(2)}) %copy-start.5) | copy-done | bytes 1605656
  31.5 0.6 all-to-all-done.pieces
  32.1 1.1 %slice.4.kv0 = bf16[4,2,256,128]{3,2,1,0:T(8,128)(2,1)S(1)} slice(bf16[4,3,256,128]{3,2,1,0:T(8,128)(2,1)} %all-to-all-done.pieces), slice={[0:4], [1:3], [0:256], [0:128]} | slice | bytes 1048576 | tf_op jit(solution)/shard_map/slice | solution.py:370
  33.2 4.0 %collective-permute-done.3.e11 = bf16[2,128,896]{2,1,0:T(8,128)(2,1)} collective-permute-done((bf16[2,128,896]{2,1,0:T(8,128)(2,1)}, bf16[2,128,896]{2,1,0:T(8,128)(2,1)}, u32[]{:S(2)}, u32[]{:S(2)}) %collective-permute-start.3) | collective-permute-done | bytes 458784 | tf_op jit(solution)/shard_map/ppermute | solution.py:358
  37.2 3.4 %collective-permute-done.4.e31 = bf16[2,128,896]{2,1,0:T(8,128)(2,1)} collective-permute-done((bf16[2,128,896]{2,1,0:T(8,128)(2,1)}, bf16[2,128,896]{2,1,0:T(8,128)(2,1)}, u32[]{:S(2)}, u32[]{:S(2)}) %collective-permute-start.4) | collective-permute-done | bytes 458784 | tf_op jit(solution)/shard_map/ppermute | solution.py:359
  40.6 0.0 collective-permute-start.5
  40.6 3.2 %collective-permute-start.6 = (bf16[2,128,896]{2,1,0:T(8,128)(2,1)}, bf16[2,128,896]{2,1,0:T(8,128)(2,1)S(1)}, u32[]{:S(2)}, u32[]{:S(2)}) collective-permute-start(bf16[2,128,896]{2,1,0:T(8,128)(2,1)} %collective-permute-done.3.e11), channel_id=1, source_target_pairs={{0,6},{2,0},{4,2},{6,4},{1,7},{3,1},{5,3},{7,5},{8,14},{10,8},{12,... | collective-permute-start | bytes 1376264 | tf_op jit(solution)/shard_map/ppermute | solution.py:381
  43.8 0.7 collective-permute-start.10
  44.5 0.0 collective-permute-start.11
  44.5 1.5 %collective-permute-start.9 = (bf16[4,2,256,128]{3,2,1,0:T(8,128)(2,1)S(1)}, bf16[4,2,256,128]{3,2,1,0:T(8,128)(2,1)S(1)}, u32[]{:S(2)}, u32[]{:S(2)}) collective-permute-start(bf16[4,2,256,128]{3,2,1,0:T(8,128)(2,1)S(1)} %slice.4.kv0), channel_id=1, source_target_pairs={{0,8},{8,0},{1,9},{9,1},{2,10},{10,2},{3,11},{11,3},{4,12},{12,4},... | collective-permute-start | bytes 1572872 | tf_op jit(solution)/shard_map/ppermute | solution.py:375
  46.0 0.9 copy-done.8
  46.9 1.2 %copy-done.10 = bf16[896,512]{1,0:T(8,128)(2,1)S(1)} copy-done((bf16[896,512]{1,0:T(8,128)(2,1)S(1)}, bf16[896,512]{1,0:T(8,128)(2,1)}, u32[]{:S(2)}) %copy-start.10) | copy-done | bytes 917528
  48.1 1.2 %copy-done.11 = bf16[896,512]{1,0:T(8,128)(2,1)S(1)} copy-done((bf16[896,512]{1,0:T(8,128)(2,1)S(1)}, bf16[896,512]{1,0:T(8,128)(2,1)}, u32[]{:S(2)}) %copy-start.11) | copy-done | bytes 917528
  49.3 1.1 %shard_map.152 = (bf16[896,1024]{1,0:T(8,128)(2,1)S(1)}, bf16[1024,896]{1,0:T(8,128)(2,1)S(1)}, bf16[4,512,256]{2,1,0:T(8,128)(2,1)S(1)}, bf16[4,512,256]{2,1,0:T(8,128)(2,1)S(1)}) custom-call(bf16[896,512]{1,0:T(8,128)(2,1)S(1)} %copy-done.10, bf16[896,512]{1,0:T(8,128)(2,1)S(1)} %copy-done.11, bf16[256,512]{1,0:T(8,128)(2,1)S(1)} %copy-done.7, ...), custom_call_target="tpu_custom_call" | custom-call | tf_op jit(solution)/shard_map/pallas_call | solution.py:384
  50.4 1.4 %collective-permute-done.5.e20 = bf16[2,128,896]{2,1,0:T(8,128)(2,1)S(1)} collective-permute-done((bf16[2,128,896]{2,1,0:T(8,128)(2,1)}, bf16[2,128,896]{2,1,0:T(8,128)(2,1)S(1)}, u32[]{:S(2)}, u32[]{:S(2)}) %collective-permute-start.5) | collective-permute-done | bytes 458784 | tf_op jit(solution)/shard_map/ppermute | solution.py:380
  51.9 0.0 collective-permute-done.6.e21
  51.9 8.9 %shard_map.153 = (f32[256,512]{1,0:T(8,128)S(1)}, bf16[2,128,896]{2,1,0:T(8,128)(2,1)S(1)}, bf16[2,128,896]{2,1,0:T(8,128)(2,1)S(1)}, bf16[2,128,896]{2,1,0:T(8,...) custom-call(s32[2,4]{1,0:T(2,128)S(1)} %bitcast.2, ...), custom_call_target="tpu_custom_call" | custom-call | tf_op jit(solution)/shard_map/pallas_call | solution.py:392
  60.8 3.0 %collective-permute-start.7 = (bf16[2,128,896]{2,1,0:T(8,128)(2,1)S(1)}, bf16[2,128,896]{2,1,0:T(8,128)(2,1)S(1)}, u32[]{:S(2)}, u32[]{:S(2)}) collective-permute-start(bf16[2,128,896]{2,1,0:T(8,128)(2,1)S(1)} %get-tuple-element.86), channel_id=1, source_target_pairs={{0,6},{2,0},{4,2},{6,4},{1,7},{3,1},{5,3},{7,5},{8,14},{10,8},{12,... | collective-permute-start | bytes 1376264 | tf_op jit(solution)/shard_map/ppermute | solution.py:426
  63.9 0.0 collective-permute-start.8
  63.9 0.0 collective-permute-done.10.kv2
  63.9 0.1 collective-permute-done.11.kv3
  64.0 0.0 collective-permute-done.9.kv1
  64.0 6.8 %shard_map.154 = (bf16[256,128]{1,0:T(8,128)(2,1)S(1)}, bf16[256,128]{1,0:T(8,128)(2,1)S(1)}, bf16[256,128]{1,0:T(8,128)(2,1)S(1)}, bf16[256,128]{1,0:T(8,128)(2,1)S(1)}) custom-call(bf16[4,3,256,128]{3,2,1,0:T(8,128)(2,1)} %all-to-all-done.pieces, bf16[4,2,256,128]{3,2,1,0:T(8,128)(2,1)S(1)} %slice.4.kv0, ...), custom_call_target="tpu_custom_call" | custom-call | tf_op jit(solution)/shard_map/pallas_call | solution.py:429
  70.8 1.1 %collective-permute-done.7 = bf16[2,128,896]{2,1,0:T(8,128)(2,1)S(1)} collective-permute-done((bf16[2,128,896]{2,1,0:T(8,128)(2,1)S(1)}, bf16[2,128,896]{2,1,0:T(8,128)(2,1)S(1)}, u32[]{:S(2)}, u32[]{:S(2)}) %collective-permute-start.7) | collective-permute-done | bytes 458784 | tf_op jit(solution)/shard_map/ppermute | solution.py:426
  71.9 1.6 %collective-permute-done.8 = bf16[2,128,896]{2,1,0:T(8,128)(2,1)S(1)} collective-permute-done((bf16[2,128,896]{2,1,0:T(8,128)(2,1)S(1)}, bf16[2,128,896]{2,1,0:T(8,128)(2,1)S(1)}, u32[]{:S(2)}, u32[]{:S(2)}) %collective-permute-start.8) | collective-permute-done | bytes 458784 | tf_op jit(solution)/shard_map/ppermute | solution.py:427
  73.5 0.1 add_convert_fusion.2
  73.7 0.5 collective-permute-start.12
  74.1 1.6 %collective-permute-start.13 = (bf16[2,128,896]{2,1,0:T(8,128)(2,1)S(1)}, bf16[2,128,896]{2,1,0:T(8,128)(2,1)S(1)}, u32[]{:S(2)}, u32[]{:S(2)}) collective-permute-start(bf16[2,128,896]{2,1,0:T(8,128)(2,1)S(1)} %get-tuple-element.100), channel_id=1, source_target_pairs={{0,2},{2,4},{4,6},{6,0},{1,3},{3,5},{5,7},{7,1},{8,10},{10,12},{12... | collective-permute-start | bytes 1376264 | tf_op jit(solution)/shard_map/ppermute | solution.py:442
  75.8 2.8 %collective-permute-start.14 = (bf16[256,128]{1,0:T(8,128)(2,1)S(1)}, bf16[256,128]{1,0:T(8,128)(2,1)S(1)}, u32[]{:S(2)}, u32[]{:S(2)}) collective-permute-start(bf16[256,128]{1,0:T(8,128)(2,1)S(1)} %get-tuple-element.105), channel_id=1, source_target_pairs={{0,96},{32,0},{64,32},{96,64},{1,97},{33,1},{65,33},{97,65},{2,98}... | collective-permute-start | bytes 196616 | tf_op jit(solution)/shard_map/ppermute | solution.py:440
  78.5 0.8 collective-permute-start.15
  79.3 0.9 collective-permute-start.16
  80.3 0.1 add_convert_fusion.1
  80.4 0.2 collective-permute-done.14.s1
  80.6 3.7 %collective-permute-done.15.s2 = bf16[256,128]{1,0:T(8,128)(2,1)S(1)} collective-permute-done((bf16[256,128]{1,0:T(8,128)(2,1)S(1)}, bf16[256,128]{1,0:T(8,128)(2,1)S(1)}, u32[]{:S(2)}, u32[]{:S(2)}) %collective-permute-start.15) | collective-permute-done | bytes 65568 | tf_op jit(solution)/shard_map/ppermute | solution.py:440
  84.3 0.7 collective-permute-done.16.s3
  85.0 0.3 collective-permute-done.12
  85.3 1.5 %collective-permute-done.13 = bf16[2,128,896]{2,1,0:T(8,128)(2,1)S(1)} collective-permute-done((bf16[2,128,896]{2,1,0:T(8,128)(2,1)S(1)}, bf16[2,128,896]{2,1,0:T(8,128)(2,1)S(1)}, u32[]{:S(2)}, u32[]{:S(2)}) %collective-permute-start.13) | collective-permute-done | bytes 458784 | tf_op jit(solution)/shard_map/ppermute | solution.py:442
  86.9 0.2 add_convert_fusion
  87.0 1.3 %collective-permute-start.19 = (bf16[2,128,896]{2,1,0:T(8,128)(2,1)S(1)}, bf16[2,128,896]{2,1,0:T(8,128)(2,1)S(1)}, u32[]{:S(2)}, u32[]{:S(2)}) collective-permute-start(bf16[2,128,896]{2,1,0:T(8,128)(2,1)S(1)} %add_convert_fusion), channel_id=1, source_target_pairs={{0,1},{1,0},{2,3},{3,2},{4,5},{5,4},{6,7},{7,6},{8,9},{9,8},{10,11... | collective-permute-start | bytes 1376264 | tf_op jit(solution)/shard_map/ppermute | solution.py:446
  88.3 0.2 collective-permute-start.17
  88.5 3.0 %collective-permute-start.18 = (bf16[2,128,896]{2,1,0:T(8,128)(2,1)S(1)}, bf16[2,128,896]{2,1,0:T(8,128)(2,1)S(1)}, u32[]{:S(2)}, u32[]{:S(2)}) collective-permute-start(bf16[2,128,896]{2,1,0:T(8,128)(2,1)S(1)} %get-tuple-element.114), channel_id=1, source_target_pairs={{0,6},{2,0},{4,2},{6,4},{1,7},{3,1},{5,3},{7,5},{8,14},{10,8},{12,... | collective-permute-start | bytes 1376264 | tf_op jit(solution)/shard_map/ppermute | solution.py:448
  91.6 0.8 shard_map.155
  92.3 6.8 %collective-permute-done.19.d3 = bf16[2,128,896]{2,1,0:T(8,128)(2,1)S(1)} collective-permute-done((bf16[2,128,896]{2,1,0:T(8,128)(2,1)S(1)}, bf16[2,128,896]{2,1,0:T(8,128)(2,1)S(1)}, u32[]{:S(2)}, u32[]{:S(2)}) %collective-permute-start.19) | collective-permute-done | bytes 458784 | tf_op jit(solution)/shard_map/ppermute | solution.py:446
  99.2 0.5 collective-permute-done.17.d1
  99.7 0.0 collective-permute-done.18.d2
  99.8 3.2 %shard_map.156 = f32[2,128,896]{2,1,0:T(8,128)} custom-call(bf16[2,128,896]{2,1,0:T(8,128)(2,1)S(1)} %get-tuple-element.112.d0, bf16[2,128,896]{2,1,0:T(8,128)(2,1)S(1)} %collective-permute-done.17.d1, bf16[2,128,896]{2,1,0:T(8,128)(2,1)S(1)} %collective-permute-done.18.d2, bf16[2,128,896]{2,1,0:T(8,128)(2,1)S(1)} %collective-permute-done.19.d3, ...), custom_call_target="tpu_custom_call" | custom-call | tf_op jit(solution)/shard_map/pallas_call | solution.py:450
  (30 shorter events, 0.1 us)
Async XLA Ops:
  0.6 14.2 %copy-start.14 = (bf16[256,512]{1,0:T(8,128)(2,1)S(1)}, bf16[256,512]{1,0:T(8,128)(2,1)}, u32[]{:S(2)}) copy-start(bf16[256,512]{1,0:T(8,128)(2,1)} %q_ref) | copy-start | bytes 786436
  0.6 14.1 %copy-start.15 = (bf16[256,512]{1,0:T(8,128)(2,1)S(1)}, bf16[256,512]{1,0:T(8,128)(2,1)}, u32[]{:S(2)}) copy-start(bf16[256,512]{1,0:T(8,128)(2,1)} %k_ref) | copy-start | bytes 786436
  0.7 14.1 %copy-start.16 = (bf16[256,512]{1,0:T(8,128)(2,1)S(1)}, bf16[256,512]{1,0:T(8,128)(2,1)}, u32[]{:S(2)}) copy-start(bf16[256,512]{1,0:T(8,128)(2,1)} %v_ref) | copy-start | bytes 786436
  0.7 27.6 %copy-start.1 = (bf16[896,896]{1,0:T(8,128)(2,1)S(1)}, bf16[896,896]{1,0:T(8,128)(2,1)}, u32[]{:S(2)}) copy-start(bf16[896,896]{1,0:T(8,128)(2,1)} %wo) | copy-start | bytes 4816900
  7.4 20.9 %copy-start = (bf16[896,896]{1,0:T(8,128)(2,1)S(1)}, bf16[896,896]{1,0:T(8,128)(2,1)}, u32[]{:S(2)}) copy-start(bf16[896,896]{1,0:T(8,128)(2,1)} %wq) | copy-start | bytes 4816900
  7.4 14.2 %collective-permute-start = (bf16[2,128,896]{2,1,0:T(8,128)(2,1)}, bf16[2,128,896]{2,1,0:T(8,128)(2,1)}, u32[]{:S(2)}, u32[]{:S(2)}) collective-permute-start(bf16[2,128,896]{2,1,0:T(8,128)(2,1)} %get-tuple-element.62.e00), channel_id=1, source_target_pairs={{0,1},{1,0},{2,3},{3,2},{4,5},{5,4},{6,7},{7,6},{8,9},{9,8},{10,11... | collective-permute-start | bytes 1376264 | tf_op jit(solution)/shard_map/ppermute | solution.py:344
  10.7 14.6 %collective-permute-start.1 = (bf16[2,128,896]{2,1,0:T(8,128)(2,1)}, bf16[2,128,896]{2,1,0:T(8,128)(2,1)}, u32[]{:S(2)}, u32[]{:S(2)}) collective-permute-start(bf16[2,128,896]{2,1,0:T(8,128)(2,1)} %get-tuple-element.62.e00), channel_id=1, source_target_pairs={{0,2},{2,4},{4,6},{6,0},{1,3},{3,5},{5,7},{7,1},{8,10},{10,12},{12... | collective-permute-start | bytes 1376264 | tf_op jit(solution)/shard_map/ppermute | solution.py:345
  12.7 12.7 %collective-permute-start.2 = (bf16[2,128,896]{2,1,0:T(8,128)(2,1)}, bf16[2,128,896]{2,1,0:T(8,128)(2,1)}, u32[]{:S(2)}, u32[]{:S(2)}) collective-permute-start(bf16[2,128,896]{2,1,0:T(8,128)(2,1)} %get-tuple-element.62.e00), channel_id=1, source_target_pairs={{0,6},{2,0},{4,2},{6,4},{1,7},{3,1},{5,3},{7,5},{8,14},{10,8},{12,... | collective-permute-start | bytes 1376264 | tf_op jit(solution)/shard_map/ppermute | solution.py:346
  14.9 0.9 copy-start.2
  15.8 16.3 %all-to-all-start = ((bf16[4,3,256,128]{3,2,1,0:T(8,128)(2,1)}), bf16[4,3,256,128]{3,2,1,0:T(8,128)(2,1)}, u32[]{:S(2)}, u32[]{:S(2)}) async-start(bf16[4,3,256,128]{3,2,1,0:T(8,128)(2,1)} %copy-done.2), calls=%async_computation | async-start | bytes 1572864 | tf_op jit(solution)/shard_map/all_to_all | solution.py:355
  20.1 25.9 %copy-start.7 = (bf16[256,512]{1,0:T(8,128)(2,1)S(1)}, bf16[256,512]{1,0:T(8,128)(2,1)}, u32[]{:S(2)}) copy-start(bf16[256,512]{1,0:T(8,128)(2,1)} %rest_3_.1) | copy-start | bytes 786436
  25.4 11.8 %collective-permute-start.3 = (bf16[2,128,896]{2,1,0:T(8,128)(2,1)}, bf16[2,128,896]{2,1,0:T(8,128)(2,1)}, u32[]{:S(2)}, u32[]{:S(2)}) collective-permute-start(bf16[2,128,896]{2,1,0:T(8,128)(2,1)} %collective-permute-done.e01), channel_id=1, source_target_pairs={{0,6},{2,0},{4,2},{6,4},{1,7},{3,1},{5,3},{7,5},{8,14},{10,8},{12,... | collective-permute-start | bytes 1376264 | tf_op jit(solution)/shard_map/ppermute | solution.py:358
  28.3 12.3 %collective-permute-start.4 = (bf16[2,128,896]{2,1,0:T(8,128)(2,1)}, bf16[2,128,896]{2,1,0:T(8,128)(2,1)}, u32[]{:S(2)}, u32[]{:S(2)}) collective-permute-start(bf16[2,128,896]{2,1,0:T(8,128)(2,1)} %collective-permute-done.e01), channel_id=1, source_target_pairs={{0,2},{2,4},{4,6},{6,0},{1,3},{3,5},{5,7},{7,1},{8,10},{10,12},{12... | collective-permute-start | bytes 1376264 | tf_op jit(solution)/shard_map/ppermute | solution.py:359
  29.2 1.2 %copy-start.3 = (bf16[896,896]{1,0:T(8,128)(2,1)}, bf16[896,896]{1,0:T(8,128)(2,1)S(1)}, u32[]{:S(2)}) copy-start(bf16[896,896]{1,0:T(8,128)(2,1)S(1)} %get-tuple-element.121.wq) | copy-start | bytes 4816900
  30.4 1.2 %copy-start.5 = (bf16[896,896]{1,0:T(8,128)(2,1)}, bf16[896,896]{1,0:T(8,128)(2,1)S(1)}, u32[]{:S(2)}) copy-start(bf16[896,896]{1,0:T(8,128)(2,1)S(1)} %get-tuple-element.118.wo) | copy-start | bytes 4816900
  31.5 20.4 %copy-start.9 = (bf16[256,512]{1,0:T(8,128)(2,1)S(1)}, bf16[256,512]{1,0:T(8,128)(2,1)}, u32[]{:S(2)}) copy-start(bf16[256,512]{1,0:T(8,128)(2,1)} %rest_4_.1) | copy-start | bytes 786436
  31.5 20.4 %copy-start.12 = (bf16[2,128,896]{2,1,0:T(8,128)(2,1)S(1)}, bf16[2,128,896]{2,1,0:T(8,128)(2,1)}, u32[]{:S(2)}) copy-start(bf16[2,128,896]{2,1,0:T(8,128)(2,1)} %get-tuple-element.62.e00) | copy-start | bytes 1376260
  31.5 20.4 %copy-start.19 = (s32[4,2]{0,1:T(2,128)S(1)}, s32[4,2]{0,1:T(2,128)}, u32[]{:S(2)}) copy-start(s32[4,2]{0,1:T(2,128)} %param.22) | copy-start | bytes 100
  40.6 11.3 %collective-permute-start.5 = (bf16[2,128,896]{2,1,0:T(8,128)(2,1)}, bf16[2,128,896]{2,1,0:T(8,128)(2,1)S(1)}, u32[]{:S(2)}, u32[]{:S(2)}) collective-permute-start(bf16[2,128,896]{2,1,0:T(8,128)(2,1)} %collective-permute-done.1.e30), channel_id=1, source_target_pairs={{0,2},{2,4},{4,6},{6,0},{1,3},{3,5},{5,7},{7,1},{8,10},{10,12},{12... | collective-permute-start | bytes 1376264 | tf_op jit(solution)/shard_map/ppermute | solution.py:380
  40.6 11.3 %collective-permute-start.6 = (bf16[2,128,896]{2,1,0:T(8,128)(2,1)}, bf16[2,128,896]{2,1,0:T(8,128)(2,1)S(1)}, u32[]{:S(2)}, u32[]{:S(2)}) collective-permute-start(bf16[2,128,896]{2,1,0:T(8,128)(2,1)} %collective-permute-done.3.e11), channel_id=1, source_target_pairs={{0,6},{2,0},{4,2},{6,4},{1,7},{3,1},{5,3},{7,5},{8,14},{10,8},{12,... | collective-permute-start | bytes 1376264 | tf_op jit(solution)/shard_map/ppermute | solution.py:381
  43.8 20.0 %collective-permute-start.10 = (bf16[4,2,256,128]{3,2,1,0:T(8,128)(2,1)S(1)}, bf16[4,2,256,128]{3,2,1,0:T(8,128)(2,1)S(1)}, u32[]{:S(2)}, u32[]{:S(2)}) collective-permute-start(bf16[4,2,256,128]{3,2,1,0:T(8,128)(2,1)S(1)} %slice.4.kv0), channel_id=1, source_target_pairs={{0,16},{16,0},{1,17},{17,1},{2,18},{18,2},{3,19},{19,3},{4,20},{20... | collective-permute-start | bytes 1572872 | tf_op jit(solution)/shard_map/ppermute | solution.py:376
  44.5 19.5 %collective-permute-start.11 = (bf16[4,2,256,128]{3,2,1,0:T(8,128)(2,1)S(1)}, bf16[4,2,256,128]{3,2,1,0:T(8,128)(2,1)S(1)}, u32[]{:S(2)}, u32[]{:S(2)}) collective-permute-start(bf16[4,2,256,128]{3,2,1,0:T(8,128)(2,1)S(1)} %slice.4.kv0), channel_id=1, source_target_pairs={{0,24},{8,16},{16,8},{24,0},{1,25},{9,17},{17,9},{25,1},{2,26},{10... | collective-permute-start | bytes 1572872 | tf_op jit(solution)/shard_map/ppermute | solution.py:377
  44.5 19.5 %collective-permute-start.9 = (bf16[4,2,256,128]{3,2,1,0:T(8,128)(2,1)S(1)}, bf16[4,2,256,128]{3,2,1,0:T(8,128)(2,1)S(1)}, u32[]{:S(2)}, u32[]{:S(2)}) collective-permute-start(bf16[4,2,256,128]{3,2,1,0:T(8,128)(2,1)S(1)} %slice.4.kv0), channel_id=1, source_target_pairs={{0,8},{8,0},{1,9},{9,1},{2,10},{10,2},{3,11},{11,3},{4,12},{12,4},... | collective-permute-start | bytes 1572872 | tf_op jit(solution)/shard_map/ppermute | solution.py:375
  46.0 1.0 copy-start.8
  46.9 1.2 %copy-start.10 = (bf16[896,512]{1,0:T(8,128)(2,1)S(1)}, bf16[896,512]{1,0:T(8,128)(2,1)}, u32[]{:S(2)}) copy-start(bf16[896,512]{1,0:T(8,128)(2,1)} %kw) | copy-start | bytes 2752516
  48.1 1.2 %copy-start.11 = (bf16[896,512]{1,0:T(8,128)(2,1)S(1)}, bf16[896,512]{1,0:T(8,128)(2,1)}, u32[]{:S(2)}) copy-start(bf16[896,512]{1,0:T(8,128)(2,1)} %vw) | copy-start | bytes 2752516
  60.8 11.1 %collective-permute-start.7 = (bf16[2,128,896]{2,1,0:T(8,128)(2,1)S(1)}, bf16[2,128,896]{2,1,0:T(8,128)(2,1)S(1)}, u32[]{:S(2)}, u32[]{:S(2)}) collective-permute-start(bf16[2,128,896]{2,1,0:T(8,128)(2,1)S(1)} %get-tuple-element.86), channel_id=1, source_target_pairs={{0,6},{2,0},{4,2},{6,4},{1,7},{3,1},{5,3},{7,5},{8,14},{10,8},{12,... | collective-permute-start | bytes 1376264 | tf_op jit(solution)/shard_map/ppermute | solution.py:426
  63.9 9.7 %collective-permute-start.8 = (bf16[2,128,896]{2,1,0:T(8,128)(2,1)S(1)}, bf16[2,128,896]{2,1,0:T(8,128)(2,1)S(1)}, u32[]{:S(2)}, u32[]{:S(2)}) collective-permute-start(bf16[2,128,896]{2,1,0:T(8,128)(2,1)S(1)} %get-tuple-element.87), channel_id=1, source_target_pairs={{0,2},{2,4},{4,6},{6,0},{1,3},{3,5},{5,7},{7,1},{8,10},{10,12},{12... | collective-permute-start | bytes 1376264 | tf_op jit(solution)/shard_map/ppermute | solution.py:427
  73.7 11.7 %collective-permute-start.12 = (bf16[2,128,896]{2,1,0:T(8,128)(2,1)S(1)}, bf16[2,128,896]{2,1,0:T(8,128)(2,1)S(1)}, u32[]{:S(2)}, u32[]{:S(2)}) collective-permute-start(bf16[2,128,896]{2,1,0:T(8,128)(2,1)S(1)} %add_convert_fusion.2), channel_id=1, source_target_pairs={{0,6},{2,0},{4,2},{6,4},{1,7},{3,1},{5,3},{7,5},{8,14},{10,8},{12,... | collective-permute-start | bytes 1376264 | tf_op jit(solution)/shard_map/ppermute | solution.py:441
  74.1 12.7 %collective-permute-start.13 = (bf16[2,128,896]{2,1,0:T(8,128)(2,1)S(1)}, bf16[2,128,896]{2,1,0:T(8,128)(2,1)S(1)}, u32[]{:S(2)}, u32[]{:S(2)}) collective-permute-start(bf16[2,128,896]{2,1,0:T(8,128)(2,1)S(1)} %get-tuple-element.100), channel_id=1, source_target_pairs={{0,2},{2,4},{4,6},{6,0},{1,3},{3,5},{5,7},{7,1},{8,10},{10,12},{12... | collective-permute-start | bytes 1376264 | tf_op jit(solution)/shard_map/ppermute | solution.py:442
  75.8 4.8 %collective-permute-start.14 = (bf16[256,128]{1,0:T(8,128)(2,1)S(1)}, bf16[256,128]{1,0:T(8,128)(2,1)S(1)}, u32[]{:S(2)}, u32[]{:S(2)}) collective-permute-start(bf16[256,128]{1,0:T(8,128)(2,1)S(1)} %get-tuple-element.105), channel_id=1, source_target_pairs={{0,96},{32,0},{64,32},{96,64},{1,97},{33,1},{65,33},{97,65},{2,98}... | collective-permute-start | bytes 196616 | tf_op jit(solution)/shard_map/ppermute | solution.py:440
  78.5 5.8 %collective-permute-start.15 = (bf16[256,128]{1,0:T(8,128)(2,1)S(1)}, bf16[256,128]{1,0:T(8,128)(2,1)S(1)}, u32[]{:S(2)}, u32[]{:S(2)}) collective-permute-start(bf16[256,128]{1,0:T(8,128)(2,1)S(1)} %get-tuple-element.106), channel_id=1, source_target_pairs={{0,64},{32,96},{64,0},{96,32},{1,65},{33,97},{65,1},{97,33},{2,66}... | collective-permute-start | bytes 196616 | tf_op jit(solution)/shard_map/ppermute | solution.py:440
  79.3 5.7 %collective-permute-start.16 = (bf16[256,128]{1,0:T(8,128)(2,1)S(1)}, bf16[256,128]{1,0:T(8,128)(2,1)S(1)}, u32[]{:S(2)}, u32[]{:S(2)}) collective-permute-start(bf16[256,128]{1,0:T(8,128)(2,1)S(1)} %get-tuple-element.107), channel_id=1, source_target_pairs={{0,32},{32,64},{64,96},{96,0},{1,33},{33,65},{65,97},{97,1},{2,34}... | collective-permute-start | bytes 196616 | tf_op jit(solution)/shard_map/ppermute | solution.py:440
  80.3 19.5 %copy-start.6 = (bf16[896,896]{1,0:T(8,128)(2,1)S(1)}, bf16[896,896]{1,0:T(8,128)(2,1)}, u32[]{:S(2)}) copy-start(bf16[896,896]{1,0:T(8,128)(2,1)} %copy-done.5) | copy-start | bytes 4816900
  80.4 19.4 %copy-start.4 = (bf16[896,896]{1,0:T(8,128)(2,1)S(1)}, bf16[896,896]{1,0:T(8,128)(2,1)}, u32[]{:S(2)}) copy-start(bf16[896,896]{1,0:T(8,128)(2,1)} %copy-done.3) | copy-start | bytes 4816900
  80.4 19.3 %copy-start.13 = (f32[2,256,128]{2,1,0:T(8,128)S(1)}, f32[2,256,128]{2,1,0:T(8,128)}, u32[]{:S(2)}) copy-start(f32[2,256,128]{2,1,0:T(8,128)} %get-tuple-element.63.wt) | copy-start | bytes 786436
  80.4 19.3 %copy-start.17 = (bf16[2,64,896]{2,1,0:T(8,128)(2,1)S(1)}, bf16[2,64,896]{2,1,0:T(8,128)(2,1)}, u32[]{:S(2)}) copy-start(bf16[2,64,896]{2,1,0:T(8,128)(2,1)} %get-tuple-element.120.ek) | copy-start | bytes 688132
  80.4 19.3 %copy-start.18 = (bf16[2,64,896]{2,1,0:T(8,128)(2,1)S(1)}, bf16[2,64,896]{2,1,0:T(8,128)(2,1)}, u32[]{:S(2)}) copy-start(bf16[2,64,896]{2,1,0:T(8,128)(2,1)} %get-tuple-element.119.ev) | copy-start | bytes 688132
  87.0 12.2 %collective-permute-start.19 = (bf16[2,128,896]{2,1,0:T(8,128)(2,1)S(1)}, bf16[2,128,896]{2,1,0:T(8,128)(2,1)S(1)}, u32[]{:S(2)}, u32[]{:S(2)}) collective-permute-start(bf16[2,128,896]{2,1,0:T(8,128)(2,1)S(1)} %add_convert_fusion), channel_id=1, source_target_pairs={{0,1},{1,0},{2,3},{3,2},{4,5},{5,4},{6,7},{7,6},{8,9},{9,8},{10,11... | collective-permute-start | bytes 1376264 | tf_op jit(solution)/shard_map/ppermute | solution.py:446
  88.3 11.4 %collective-permute-start.17 = (bf16[2,128,896]{2,1,0:T(8,128)(2,1)S(1)}, bf16[2,128,896]{2,1,0:T(8,128)(2,1)S(1)}, u32[]{:S(2)}, u32[]{:S(2)}) collective-permute-start(bf16[2,128,896]{2,1,0:T(8,128)(2,1)S(1)} %add_convert_fusion.1), channel_id=1, source_target_pairs={{0,2},{2,4},{4,6},{6,0},{1,3},{3,5},{5,7},{7,1},{8,10},{10,12},{12... | collective-permute-start | bytes 1376264 | tf_op jit(solution)/shard_map/ppermute | solution.py:447
  88.5 11.2 %collective-permute-start.18 = (bf16[2,128,896]{2,1,0:T(8,128)(2,1)S(1)}, bf16[2,128,896]{2,1,0:T(8,128)(2,1)S(1)}, u32[]{:S(2)}, u32[]{:S(2)}) collective-permute-start(bf16[2,128,896]{2,1,0:T(8,128)(2,1)S(1)} %get-tuple-element.114), channel_id=1, source_target_pairs={{0,6},{2,0},{4,2},{6,4},{1,7},{3,1},{5,3},{7,5},{8,14},{10,8},{12,... | collective-permute-start | bytes 1376264 | tf_op jit(solution)/shard_map/ppermute | solution.py:448
where the time goes:
time: 103 us
  starting transfers between devices  34.1 us (33%)
  waiting for transfers between devices  31.3 us (30%)
  Pallas kernels  28.6 us (28%)
  local copies, waits for them, and re-layouts  7.65 us (7%)
    pallas_call x1, Pallas kernels, local(): call(cross_kernel, out_shape=[struct((rows, width), F32)] + [struct((slot...  8.95 us
    ppermute x1, waiting for transfers between devices, local(): other = lax.ppermute(theirs, 'yh', shift(2, 1))  6.83 us
    pallas_call x1, Pallas kernels, local(): call(attend_kernel, out_shape=[struct((rows, HSIZE), BF16)] * NX, in_spec...  6.82 us
    pallas_call x1, Pallas kernels, local(): call(encode_kernel, mib=56, out_shape=[struct((slots, nl, ew), BF16), str...  6.69 us
    unnamed x40, local copies, waits for them, and re-layouts  6.57 us
    ppermute x3, waiting for transfers between devices, local(): lax.ppermute(outs[d], 'x', shift(NX, -d))  4.58 us
    ppermute x3, starting transfers between devices, local(): lax.ppermute(outs[d], 'x', shift(NX, -d))  4.49 us
    all_to_all x1, starting transfers between devices, local(): pieces = lax.all_to_all(packed, 'x', 0, 0)  4.28 us
  transfers between devices with their start and end apart: 21, of which 16 were waited for; matrix products, arithmetic and copies ran while one was open for 1% of the time, Pallas kernels for 18%

commit v1 on v0

--- a/solution.py
+++ b/solution.py
@@ -129,17 +129,21 @@
     ids, nb_h, ctx_h, wq_h, wk_h, wv_h, wo_h, enc, wt, ek_out, ev_out, *scratch
 ):
     nb, ctx, wq, wk, wv, wo, sems = scratch
-    both = ((nb_h, nb), (wq_h, wq), (ctx_h, ctx), (wk_h, wk), (wv_h, wv), (wo_h, wo))
+    slots, rows, width = nb.shape
+    each = width // EHEADS
+    both = [(nb_h, nb)]
+    for i in range(EHEADS):
+        part = slice(i * each, (i + 1) * each)
+        both.append((wq_h.at[part], wq.at[part]))
+    both += [(ctx_h, ctx), (wk_h, wk), (wv_h, wv), (wo_h, wo)]
     copies = [pltpu.make_async_copy(a, b, sems.at[i]) for i, (a, b) in enumerate(both)]
     for c in copies:
         c.start()
-    slots, rows, width = nb.shape
-    each = width // EHEADS
-    copies[0].wait()
+    for c in copies[:5]:
+        c.wait()
     x = nb[...].reshape(slots * rows, width)
-    copies[1].wait()
     eq = mm(x, wq[...]).astype(BF16)
-    copies[2].wait()
+    copies[5].wait()
     contexts = []
     for t in range(slots):
         mine = (lax.axis_index("z") * 2 + lax.axis_index("yh")) * slots + t
@@ -148,23 +152,27 @@
             span = jnp.where((ids[0, c] == mine) | (ids[1, c] == mine), c, span)
         contexts.append(ctx[pl.ds(pl.multiple_of(span * CL, CL), CL), :])
     m = jnp.concatenate(contexts, axis=0)
-    copies[3].wait()
+    copies[6].wait()
     ek = mm(m, wk[...]).astype(BF16)
-    copies[4].wait()
+    scores = [
+        mm_nt(head_rows(ek[t * CL : (t + 1) * CL]), eq[t * rows : (t + 1) * rows])
+        for t in range(slots)
+    ]
+    copies[7].wait()
     ev = mm(m, wv[...]).astype(BF16)
+    copies[8].wait()
+    probs = []
+    for s in scores:
+        s = (s * (1.0 / math.sqrt(each))).reshape(EHEADS, CL, rows)
+        p = jnp.exp(s - jnp.max(s, axis=1, keepdims=True))
+        probs.append((p * (1.0 / jnp.sum(p, axis=1, keepdims=True))).reshape(EHEADS * CL, rows))
     mixed = []
-    for t in range(slots):
-        ek_t = ek[t * CL : (t + 1) * CL]
+    for t, w in enumerate(probs):
         ev_t = ev[t * CL : (t + 1) * CL]
-        s = mm_nt(head_rows(ek_t), eq[t * rows : (t + 1) * rows]) * (1.0 / math.sqrt(each))
-        s = s.reshape(EHEADS, CL, rows)
-        p = jnp.exp(s - jnp.max(s, axis=1, keepdims=True))
-        w = (p * (1.0 / jnp.sum(p, axis=1, keepdims=True))).reshape(EHEADS * CL, rows)
+        mixed.append(mm_tn(w.astype(BF16), head_rows(ev_t)).astype(BF16))
         wt[t] = w
-        ek_out[t] = ek_t
+        ek_out[t] = ek[t * CL : (t + 1) * CL]
         ev_out[t] = ev_t
-        mixed.append(mm_tn(w.astype(BF16), head_rows(ev_t)).astype(BF16))
-    copies[5].wait()
     out = x.astype(F32) + mm(jnp.concatenate(mixed, axis=0), wo[...])
     enc[...] = out.astype(BF16).reshape(slots, rows, width)
 
@@ -175,15 +183,16 @@
     d = (d0[...].astype(F32) + d1[...].astype(F32)) + (d2[...].astype(F32) + d3[...].astype(F32))
     d = d.reshape(slots * rows, width)
     de = mm(d.astype(BF16), wo[...]).astype(BF16)
-    back = []
-    for t in range(slots):
-        w = wt[t]
-        dw = mm_nt(head_rows(ev[t]), de[t * rows : (t + 1) * rows])
+    turned = [
+        mm_nt(head_rows(ev[t]), de[t * rows : (t + 1) * rows]) for t in range(slots)
+    ]
+    inner = []
+    for t, dw in enumerate(turned):
         dw = dw.astype(BF16).astype(F32).reshape(EHEADS, CL, rows)
-        w = w.reshape(EHEADS, CL, rows)
+        w = wt[t].reshape(EHEADS, CL, rows)
         ds = w * (dw - jnp.sum(w * dw, axis=1, keepdims=True)) * (1.0 / math.sqrt(each))
-        ds = ds.reshape(EHEADS * CL, rows).astype(BF16)
-        back.append(mm_tn(ds, head_rows(ek[t])).astype(BF16))
+        inner.append(ds.reshape(EHEADS * CL, rows).astype(BF16))
+    back = [mm_tn(ds, head_rows(ek[t])).astype(BF16) for t, ds in enumerate(inner)]
     out[...] = (d + mm(jnp.concatenate(back, axis=0), wq[...])).reshape(slots, rows, width)
 
 
@@ -244,7 +253,8 @@
 
     heads = width // HSIZE
     pair = 2 * NL
-    for half in range(2):
+
+    def project(half):
         first = half * (n_named // 2)
         e = held[first : first + n_named // 2].reshape(n_named // 2 * NL, -1)
         ckv[first * NL : (first + n_named // 2) * NL] = mm(e, kvw[...]).astype(BF16)
@@ -282,12 +292,13 @@
             def _():
                 outs[i][t] = sent[n]
 
-    ahead = scores(0)
+    project(0)
+    ahead = [scores(c) for c in range(spans // 2)]
+    project(1)
     for c in range(spans):
-        now = ahead
-        if c + 1 < spans:
-            ahead = scores(c + 1)
-        soft = soften(*now)
+        soft = soften(*ahead[c])
+        if c + spans // 2 < spans:
+            ahead.append(scores(c + spans // 2))
         if c >= 1:
             back(c - 1)
         products(c, *soft)
@@ -338,7 +349,7 @@
         out_specs=[vmem()] * 4,
         scratch_shapes=[pltpu.VMEM(neighbours.shape, BF16), pltpu.VMEM(span_ctx.shape, BF16)]
         + [pltpu.VMEM((ew, ew), BF16)] * 4
-        + [pltpu.SemaphoreType.DMA((6,))],
+        + [pltpu.SemaphoreType.DMA((9,))],
     )(ids, neighbours, span_ctx, enc_q, enc_k, enc_v, enc_o)
 
     e01 = lax.ppermute(e00, "yh", shift(2, 1))

time: 103 us -> 103 us (level)
  no operation moved by 1% of the time
where the time goes in v1:
time: 103 us; the launch traced here: 102 us
  starting transfers between devices  34 us (33%)
  waiting for transfers between devices  31.7 us (31%)
  Pallas kernels  27.7 us (27%)
  local copies, waits for them, and re-layouts  7.65 us (7%)
    pallas_call x1, Pallas kernels, local(): call(cross_kernel, out_shape=[struct((rows, width), F32)] + [struct((slot...  8.83 us
    ppermute x1, waiting for transfers between devices, local(): other = lax.ppermute(theirs, 'yh', shift(2, 1))  6.94 us
    pallas_call x1, Pallas kernels, local(): call(attend_kernel, out_shape=[struct((rows, HSIZE), BF16)] * NX, in_spec...  6.82 us
    unnamed x40, local copies, waits for them, and re-layouts  6.57 us
    pallas_call x1, Pallas kernels, local(): call(encode_kernel, mib=56, out_shape=[struct((slots, nl, ew), BF16), str...  6.26 us
    ppermute x3, waiting for transfers between devices, local(): lax.ppermute(outs[d], 'x', shift(NX, -d))  4.61 us
    ppermute x3, starting transfers between devices, local(): lax.ppermute(outs[d], 'x', shift(NX, -d))  4.39 us
    all_to_all x1, starting transfers between devices, local(): pieces = lax.all_to_all(packed, 'x', 0, 0)  4.29 us
  transfers between devices with their start and end apart: 21, of which 16 were waited for; matrix products, arithmetic and copies ran while one was open for 1% of the time, Pallas kernels for 18%

profile of v1, /device:TPU:0, one launch (start us, length us, event | category | flops | bytes accessed | tf_op | source)
XLA Modules:
  0.0 102.3 jit_solution(16682374030565692336)
XLA Ops:
  0.6 0.0 copy-start.14
  0.7 6.3 %shard_map.149 = (bf16[2,128,896]{2,1,0:T(8,128)(2,1)}, f32[2,256,128]{2,1,0:T(8,128)}, bf16[2,64,896]{2,1,0:T(8,128)(2,1)}, bf16[2,64,896]{2,1,0:T(8,128)(2,1)}) custom-call(s32[2,4]{1,0:T(2,128)} %bitcast.1, bf16[2,128,896]{2,1,0:T(8,128)(2,1)} %nb_h.1, bf16[256,896]{1,0:T(8,128)(2,1)} %ctx_h.1, bf16[896,896]{1,0:T(8,128)(2,1)} %wq, ...), custom_call_target="tpu_custom_call" | custom-call | tf_op jit(solution)/shard_map/pallas_call | solution.py:339
  6.9 0.0 copy-start
  7.0 3.3 %collective-permute-start = (bf16[2,128,896]{2,1,0:T(8,128)(2,1)}, bf16[2,128,896]{2,1,0:T(8,128)(2,1)}, u32[]{:S(2)}, u32[]{:S(2)}) collective-permute-start(bf16[2,128,896]{2,1,0:T(8,128)(2,1)} %get-tuple-element.62.e00), channel_id=1, source_target_pairs={{0,1},{1,0},{2,3},{3,2},{4,5},{5,4},{6,7},{7,6},{8,9},{9,8},{10,11... | collective-permute-start | bytes 1376264 | tf_op jit(solution)/shard_map/ppermute | solution.py:355
  10.3 1.9 %collective-permute-start.1 = (bf16[2,128,896]{2,1,0:T(8,128)(2,1)}, bf16[2,128,896]{2,1,0:T(8,128)(2,1)}, u32[]{:S(2)}, u32[]{:S(2)}) collective-permute-start(bf16[2,128,896]{2,1,0:T(8,128)(2,1)} %get-tuple-element.62.e00), channel_id=1, source_target_pairs={{0,2},{2,4},{4,6},{6,0},{1,3},{3,5},{5,7},{7,1},{8,10},{10,12},{12... | collective-permute-start | bytes 1376264 | tf_op jit(solution)/shard_map/ppermute | solution.py:356
  12.2 2.1 %collective-permute-start.2 = (bf16[2,128,896]{2,1,0:T(8,128)(2,1)}, bf16[2,128,896]{2,1,0:T(8,128)(2,1)}, u32[]{:S(2)}, u32[]{:S(2)}) collective-permute-start(bf16[2,128,896]{2,1,0:T(8,128)(2,1)} %get-tuple-element.62.e00), channel_id=1, source_target_pairs={{0,6},{2,0},{4,2},{6,4},{1,7},{3,1},{5,3},{7,5},{8,14},{10,8},{12,... | collective-permute-start | bytes 1376264 | tf_op jit(solution)/shard_map/ppermute | solution.py:357
  14.4 0.1 shard_map.150
  14.5 0.0 copy-start.2
  14.5 0.9 copy-done.2
  15.4 4.3 %all-to-all-start = ((bf16[4,3,256,128]{3,2,1,0:T(8,128)(2,1)}), bf16[4,3,256,128]{3,2,1,0:T(8,128)(2,1)}, u32[]{:S(2)}, u32[]{:S(2)}) async-start(bf16[4,3,256,128]{3,2,1,0:T(8,128)(2,1)} %copy-done.2), calls=%async_computation | async-start | bytes 1572864 | tf_op jit(solution)/shard_map/all_to_all | solution.py:366
  19.7 1.5 %collective-permute-done.e01 = bf16[2,128,896]{2,1,0:T(8,128)(2,1)} collective-permute-done((bf16[2,128,896]{2,1,0:T(8,128)(2,1)}, bf16[2,128,896]{2,1,0:T(8,128)(2,1)}, u32[]{:S(2)}, u32[]{:S(2)}) %collective-permute-start) | collective-permute-done | bytes 458784 | tf_op jit(solution)/shard_map/ppermute | solution.py:355
  21.2 3.8 %collective-permute-done.1.e30 = bf16[2,128,896]{2,1,0:T(8,128)(2,1)} collective-permute-done((bf16[2,128,896]{2,1,0:T(8,128)(2,1)}, bf16[2,128,896]{2,1,0:T(8,128)(2,1)}, u32[]{:S(2)}, u32[]{:S(2)}) %collective-permute-start.1) | collective-permute-done | bytes 458784 | tf_op jit(solution)/shard_map/ppermute | solution.py:356
  24.9 0.0 collective-permute-done.2.e10
  24.9 2.9 %collective-permute-start.3 = (bf16[2,128,896]{2,1,0:T(8,128)(2,1)}, bf16[2,128,896]{2,1,0:T(8,128)(2,1)}, u32[]{:S(2)}, u32[]{:S(2)}) collective-permute-start(bf16[2,128,896]{2,1,0:T(8,128)(2,1)} %collective-permute-done.e01), channel_id=1, source_target_pairs={{0,6},{2,0},{4,2},{6,4},{1,7},{3,1},{5,3},{7,5},{8,14},{10,8},{12,... | collective-permute-start | bytes 1376264 | tf_op jit(solution)/shard_map/ppermute | solution.py:369
  27.9 0.0 collective-permute-start.4
  27.9 0.9 shard_map.151
  28.8 1.2 %copy-done.3 = bf16[896,896]{1,0:T(8,128)(2,1)} copy-done((bf16[896,896]{1,0:T(8,128)(2,1)}, bf16[896,896]{1,0:T(8,128)(2,1)S(1)}, u32[]{:S(2)}) %copy-start.3) | copy-done | bytes 1605656
  30.0 1.2 %copy-done.5 = bf16[896,896]{1,0:T(8,128)(2,1)} copy-done((bf16[896,896]{1,0:T(8,128)(2,1)}, bf16[896,896]{1,0:T(8,128)(2,1)S(1)}, u32[]{:S(2)}) %copy-start.5) | copy-done | bytes 1605656
  31.1 0.6 all-to-all-done.pieces
  31.7 1.1 %slice.4.kv0 = bf16[4,2,256,128]{3,2,1,0:T(8,128)(2,1)S(1)} slice(bf16[4,3,256,128]{3,2,1,0:T(8,128)(2,1)} %all-to-all-done.pieces), slice={[0:4], [1:3], [0:256], [0:128]} | slice | bytes 1048576 | tf_op jit(solution)/shard_map/slice | solution.py:381
  32.8 4.0 %collective-permute-done.3.e11 = bf16[2,128,896]{2,1,0:T(8,128)(2,1)} collective-permute-done((bf16[2,128,896]{2,1,0:T(8,128)(2,1)}, bf16[2,128,896]{2,1,0:T(8,128)(2,1)}, u32[]{:S(2)}, u32[]{:S(2)}) %collective-permute-start.3) | collective-permute-done | bytes 458784 | tf_op jit(solution)/shard_map/ppermute | solution.py:369
  36.8 3.4 %collective-permute-done.4.e31 = bf16[2,128,896]{2,1,0:T(8,128)(2,1)} collective-permute-done((bf16[2,128,896]{2,1,0:T(8,128)(2,1)}, bf16[2,128,896]{2,1,0:T(8,128)(2,1)}, u32[]{:S(2)}, u32[]{:S(2)}) %collective-permute-start.4) | collective-permute-done | bytes 458784 | tf_op jit(solution)/shard_map/ppermute | solution.py:370
  40.2 0.0 collective-permute-start.5
  40.2 3.2 %collective-permute-start.6 = (bf16[2,128,896]{2,1,0:T(8,128)(2,1)}, bf16[2,128,896]{2,1,0:T(8,128)(2,1)S(1)}, u32[]{:S(2)}, u32[]{:S(2)}) collective-permute-start(bf16[2,128,896]{2,1,0:T(8,128)(2,1)} %collective-permute-done.3.e11), channel_id=1, source_target_pairs={{0,6},{2,0},{4,2},{6,4},{1,7},{3,1},{5,3},{7,5},{8,14},{10,8},{12,... | collective-permute-start | bytes 1376264 | tf_op jit(solution)/shard_map/ppermute | solution.py:392
  43.4 0.7 collective-permute-start.10
  44.1 0.0 collective-permute-start.11
  44.1 1.5 %collective-permute-start.9 = (bf16[4,2,256,128]{3,2,1,0:T(8,128)(2,1)S(1)}, bf16[4,2,256,128]{3,2,1,0:T(8,128)(2,1)S(1)}, u32[]{:S(2)}, u32[]{:S(2)}) collective-permute-start(bf16[4,2,256,128]{3,2,1,0:T(8,128)(2,1)S(1)} %slice.4.kv0), channel_id=1, source_target_pairs={{0,8},{8,0},{1,9},{9,1},{2,10},{10,2},{3,11},{11,3},{4,12},{12,4},... | collective-permute-start | bytes 1572872 | tf_op jit(solution)/shard_map/ppermute | solution.py:386
  45.6 0.9 copy-done.8
  46.5 1.2 %copy-done.10 = bf16[896,512]{1,0:T(8,128)(2,1)S(1)} copy-done((bf16[896,512]{1,0:T(8,128)(2,1)S(1)}, bf16[896,512]{1,0:T(8,128)(2,1)}, u32[]{:S(2)}) %copy-start.10) | copy-done | bytes 917528
  47.7 1.2 %copy-done.11 = bf16[896,512]{1,0:T(8,128)(2,1)S(1)} copy-done((bf16[896,512]{1,0:T(8,128)(2,1)S(1)}, bf16[896,512]{1,0:T(8,128)(2,1)}, u32[]{:S(2)}) %copy-start.11) | copy-done | bytes 917528
  48.9 1.1 %shard_map.152 = (bf16[896,1024]{1,0:T(8,128)(2,1)S(1)}, bf16[1024,896]{1,0:T(8,128)(2,1)S(1)}, bf16[4,512,256]{2,1,0:T(8,128)(2,1)S(1)}, bf16[4,512,256]{2,1,0:T(8,128)(2,1)S(1)}) custom-call(bf16[896,512]{1,0:T(8,128)(2,1)S(1)} %copy-done.10, bf16[896,512]{1,0:T(8,128)(2,1)S(1)} %copy-done.11, bf16[256,512]{1,0:T(8,128)(2,1)S(1)} %copy-done.7, ...), custom_call_target="tpu_custom_call" | custom-call | tf_op jit(solution)/shard_map/pallas_call | solution.py:395
  50.0 1.5 %collective-permute-done.5.e20 = bf16[2,128,896]{2,1,0:T(8,128)(2,1)S(1)} collective-permute-done((bf16[2,128,896]{2,1,0:T(8,128)(2,1)}, bf16[2,128,896]{2,1,0:T(8,128)(2,1)S(1)}, u32[]{:S(2)}, u32[]{:S(2)}) %collective-permute-start.5) | collective-permute-done | bytes 458784 | tf_op jit(solution)/shard_map/ppermute | solution.py:391
  51.5 0.0 collective-permute-done.6.e21
  51.5 8.8 %shard_map.153 = (f32[256,512]{1,0:T(8,128)S(1)}, bf16[2,128,896]{2,1,0:T(8,128)(2,1)S(1)}, bf16[2,128,896]{2,1,0:T(8,128)(2,1)S(1)}, bf16[2,128,896]{2,1,0:T(8,...) custom-call(s32[2,4]{1,0:T(2,128)S(1)} %bitcast.2, ...), custom_call_target="tpu_custom_call" | custom-call | tf_op jit(solution)/shard_map/pallas_call | solution.py:403
  60.3 3.0 %collective-permute-start.7 = (bf16[2,128,896]{2,1,0:T(8,128)(2,1)S(1)}, bf16[2,128,896]{2,1,0:T(8,128)(2,1)S(1)}, u32[]{:S(2)}, u32[]{:S(2)}) collective-permute-start(bf16[2,128,896]{2,1,0:T(8,128)(2,1)S(1)} %get-tuple-element.86), channel_id=1, source_target_pairs={{0,6},{2,0},{4,2},{6,4},{1,7},{3,1},{5,3},{7,5},{8,14},{10,8},{12,... | collective-permute-start | bytes 1376264 | tf_op jit(solution)/shard_map/ppermute | solution.py:437
  63.4 0.0 collective-permute-start.8
  63.4 0.0 collective-permute-done.10.kv2
  63.4 0.2 collective-permute-done.11.kv3
  63.6 0.0 collective-permute-done.9.kv1
  63.6 6.8 %shard_map.154 = (bf16[256,128]{1,0:T(8,128)(2,1)S(1)}, bf16[256,128]{1,0:T(8,128)(2,1)S(1)}, bf16[256,128]{1,0:T(8,128)(2,1)S(1)}, bf16[256,128]{1,0:T(8,128)(2,1)S(1)}) custom-call(bf16[4,3,256,128]{3,2,1,0:T(8,128)(2,1)} %all-to-all-done.pieces, bf16[4,2,256,128]{3,2,1,0:T(8,128)(2,1)S(1)} %slice.4.kv0, ...), custom_call_target="tpu_custom_call" | custom-call | tf_op jit(solution)/shard_map/pallas_call | solution.py:440
  70.4 1.0 collective-permute-done.7
  71.4 1.6 %collective-permute-done.8 = bf16[2,128,896]{2,1,0:T(8,128)(2,1)S(1)} collective-permute-done((bf16[2,128,896]{2,1,0:T(8,128)(2,1)S(1)}, bf16[2,128,896]{2,1,0:T(8,128)(2,1)S(1)}, u32[]{:S(2)}, u32[]{:S(2)}) %collective-permute-start.8) | collective-permute-done | bytes 458784 | tf_op jit(solution)/shard_map/ppermute | solution.py:438
  73.1 0.1 add_convert_fusion.2
  73.2 0.5 collective-permute-start.12
  73.7 1.6 %collective-permute-start.13 = (bf16[2,128,896]{2,1,0:T(8,128)(2,1)S(1)}, bf16[2,128,896]{2,1,0:T(8,128)(2,1)S(1)}, u32[]{:S(2)}, u32[]{:S(2)}) collective-permute-start(bf16[2,128,896]{2,1,0:T(8,128)(2,1)S(1)} %get-tuple-element.100), channel_id=1, source_target_pairs={{0,2},{2,4},{4,6},{6,0},{1,3},{3,5},{5,7},{7,1},{8,10},{10,12},{12... | collective-permute-start | bytes 1376264 | tf_op jit(solution)/shard_map/ppermute | solution.py:453
  75.3 2.7 %collective-permute-start.14 = (bf16[256,128]{1,0:T(8,128)(2,1)S(1)}, bf16[256,128]{1,0:T(8,128)(2,1)S(1)}, u32[]{:S(2)}, u32[]{:S(2)}) collective-permute-start(bf16[256,128]{1,0:T(8,128)(2,1)S(1)} %get-tuple-element.105), channel_id=1, source_target_pairs={{0,96},{32,0},{64,32},{96,64},{1,97},{33,1},{65,33},{97,65},{2,98}... | collective-permute-start | bytes 196616 | tf_op jit(solution)/shard_map/ppermute | solution.py:451
  78.0 0.9 collective-permute-start.15
  78.9 0.8 collective-permute-start.16
  79.7 0.1 add_convert_fusion.1
  79.8 0.3 collective-permute-done.14.s1
  80.1 3.6 %collective-permute-done.15.s2 = bf16[256,128]{1,0:T(8,128)(2,1)S(1)} collective-permute-done((bf16[256,128]{1,0:T(8,128)(2,1)S(1)}, bf16[256,128]{1,0:T(8,128)(2,1)S(1)}, u32[]{:S(2)}, u32[]{:S(2)}) %collective-permute-start.15) | collective-permute-done | bytes 65568 | tf_op jit(solution)/shard_map/ppermute | solution.py:451
  83.7 0.7 collective-permute-done.16.s3
  84.4 0.5 collective-permute-done.12
  85.0 1.5 %collective-permute-done.13 = bf16[2,128,896]{2,1,0:T(8,128)(2,1)S(1)} collective-permute-done((bf16[2,128,896]{2,1,0:T(8,128)(2,1)S(1)}, bf16[2,128,896]{2,1,0:T(8,128)(2,1)S(1)}, u32[]{:S(2)}, u32[]{:S(2)}) %collective-permute-start.13) | collective-permute-done | bytes 458784 | tf_op jit(solution)/shard_map/ppermute | solution.py:453
  86.5 0.2 add_convert_fusion
  86.6 1.3 %collective-permute-start.19 = (bf16[2,128,896]{2,1,0:T(8,128)(2,1)S(1)}, bf16[2,128,896]{2,1,0:T(8,128)(2,1)S(1)}, u32[]{:S(2)}, u32[]{:S(2)}) collective-permute-start(bf16[2,128,896]{2,1,0:T(8,128)(2,1)S(1)} %add_convert_fusion), channel_id=1, source_target_pairs={{0,1},{1,0},{2,3},{3,2},{4,5},{5,4},{6,7},{7,6},{8,9},{9,8},{10,11... | collective-permute-start | bytes 1376264 | tf_op jit(solution)/shard_map/ppermute | solution.py:457
  87.9 0.2 collective-permute-start.17
  88.2 3.0 %collective-permute-start.18 = (bf16[2,128,896]{2,1,0:T(8,128)(2,1)S(1)}, bf16[2,128,896]{2,1,0:T(8,128)(2,1)S(1)}, u32[]{:S(2)}, u32[]{:S(2)}) collective-permute-start(bf16[2,128,896]{2,1,0:T(8,128)(2,1)S(1)} %get-tuple-element.114), channel_id=1, source_target_pairs={{0,6},{2,0},{4,2},{6,4},{1,7},{3,1},{5,3},{7,5},{8,14},{10,8},{12,... | collective-permute-start | bytes 1376264 | tf_op jit(solution)/shard_map/ppermute | solution.py:459
  91.2 0.8 shard_map.155
  92.0 6.9 %collective-permute-done.19.d3 = bf16[2,128,896]{2,1,0:T(8,128)(2,1)S(1)} collective-permute-done((bf16[2,128,896]{2,1,0:T(8,128)(2,1)S(1)}, bf16[2,128,896]{2,1,0:T(8,128)(2,1)S(1)}, u32[]{:S(2)}, u32[]{:S(2)}) %collective-permute-start.19) | collective-permute-done | bytes 458784 | tf_op jit(solution)/shard_map/ppermute | solution.py:457
  98.9 0.5 collective-permute-done.17.d1
  99.4 0.0 collective-permute-done.18.d2
  99.4 0.0 copy-done.6
  99.5 2.8 %shard_map.156 = f32[2,128,896]{2,1,0:T(8,128)} custom-call(bf16[2,128,896]{2,1,0:T(8,128)(2,1)S(1)} %get-tuple-element.112.d0, bf16[2,128,896]{2,1,0:T(8,128)(2,1)S(1)} %collective-permute-done.17.d1, bf16[2,128,896]{2,1,0:T(8,128)(2,1)S(1)} %collective-permute-done.18.d2, bf16[2,128,896]{2,1,0:T(8,128)(2,1)S(1)} %collective-permute-done.19.d3, ...), custom_call_target="tpu_custom_call" | custom-call | tf_op jit(solution)/shard_map/pallas_call | solution.py:461
  (30 shorter events, 0.1 us)
Async XLA Ops:
  0.6 13.7 %copy-start.14 = (bf16[256,512]{1,0:T(8,128)(2,1)S(1)}, bf16[256,512]{1,0:T(8,128)(2,1)}, u32[]{:S(2)}) copy-start(bf16[256,512]{1,0:T(8,128)(2,1)} %q_ref) | copy-start | bytes 786436
  0.6 13.7 %copy-start.15 = (bf16[256,512]{1,0:T(8,128)(2,1)S(1)}, bf16[256,512]{1,0:T(8,128)(2,1)}, u32[]{:S(2)}) copy-start(bf16[256,512]{1,0:T(8,128)(2,1)} %k_ref) | copy-start | bytes 786436
  0.7 13.7 %copy-start.16 = (bf16[256,512]{1,0:T(8,128)(2,1)S(1)}, bf16[256,512]{1,0:T(8,128)(2,1)}, u32[]{:S(2)}) copy-start(bf16[256,512]{1,0:T(8,128)(2,1)} %v_ref) | copy-start | bytes 786436
  0.7 27.2 %copy-start.1 = (bf16[896,896]{1,0:T(8,128)(2,1)S(1)}, bf16[896,896]{1,0:T(8,128)(2,1)}, u32[]{:S(2)}) copy-start(bf16[896,896]{1,0:T(8,128)(2,1)} %wo) | copy-start | bytes 4816900
  6.9 20.9 %copy-start = (bf16[896,896]{1,0:T(8,128)(2,1)S(1)}, bf16[896,896]{1,0:T(8,128)(2,1)}, u32[]{:S(2)}) copy-start(bf16[896,896]{1,0:T(8,128)(2,1)} %wq) | copy-start | bytes 4816900
  7.0 14.2 %collective-permute-start = (bf16[2,128,896]{2,1,0:T(8,128)(2,1)}, bf16[2,128,896]{2,1,0:T(8,128)(2,1)}, u32[]{:S(2)}, u32[]{:S(2)}) collective-permute-start(bf16[2,128,896]{2,1,0:T(8,128)(2,1)} %get-tuple-element.62.e00), channel_id=1, source_target_pairs={{0,1},{1,0},{2,3},{3,2},{4,5},{5,4},{6,7},{7,6},{8,9},{9,8},{10,11... | collective-permute-start | bytes 1376264 | tf_op jit(solution)/shard_map/ppermute | solution.py:355
  10.3 14.6 %collective-permute-start.1 = (bf16[2,128,896]{2,1,0:T(8,128)(2,1)}, bf16[2,128,896]{2,1,0:T(8,128)(2,1)}, u32[]{:S(2)}, u32[]{:S(2)}) collective-permute-start(bf16[2,128,896]{2,1,0:T(8,128)(2,1)} %get-tuple-element.62.e00), channel_id=1, source_target_pairs={{0,2},{2,4},{4,6},{6,0},{1,3},{3,5},{5,7},{7,1},{8,10},{10,12},{12... | collective-permute-start | bytes 1376264 | tf_op jit(solution)/shard_map/ppermute | solution.py:356
  12.2 12.7 %collective-permute-start.2 = (bf16[2,128,896]{2,1,0:T(8,128)(2,1)}, bf16[2,128,896]{2,1,0:T(8,128)(2,1)}, u32[]{:S(2)}, u32[]{:S(2)}) collective-permute-start(bf16[2,128,896]{2,1,0:T(8,128)(2,1)} %get-tuple-element.62.e00), channel_id=1, source_target_pairs={{0,6},{2,0},{4,2},{6,4},{1,7},{3,1},{5,3},{7,5},{8,14},{10,8},{12,... | collective-permute-start | bytes 1376264 | tf_op jit(solution)/shard_map/ppermute | solution.py:357
  14.5 0.9 copy-start.2
  15.4 16.3 %all-to-all-start = ((bf16[4,3,256,128]{3,2,1,0:T(8,128)(2,1)}), bf16[4,3,256,128]{3,2,1,0:T(8,128)(2,1)}, u32[]{:S(2)}, u32[]{:S(2)}) async-start(bf16[4,3,256,128]{3,2,1,0:T(8,128)(2,1)} %copy-done.2), calls=%async_computation | async-start | bytes 1572864 | tf_op jit(solution)/shard_map/all_to_all | solution.py:366
  19.7 25.9 %copy-start.7 = (bf16[256,512]{1,0:T(8,128)(2,1)S(1)}, bf16[256,512]{1,0:T(8,128)(2,1)}, u32[]{:S(2)}) copy-start(bf16[256,512]{1,0:T(8,128)(2,1)} %rest_3_.1) | copy-start | bytes 786436
  24.9 11.8 %collective-permute-start.3 = (bf16[2,128,896]{2,1,0:T(8,128)(2,1)}, bf16[2,128,896]{2,1,0:T(8,128)(2,1)}, u32[]{:S(2)}, u32[]{:S(2)}) collective-permute-start(bf16[2,128,896]{2,1,0:T(8,128)(2,1)} %collective-permute-done.e01), channel_id=1, source_target_pairs={{0,6},{2,0},{4,2},{6,4},{1,7},{3,1},{5,3},{7,5},{8,14},{10,8},{12,... | collective-permute-start | bytes 1376264 | tf_op jit(solution)/shard_map/ppermute | solution.py:369
  27.9 12.3 %collective-permute-start.4 = (bf16[2,128,896]{2,1,0:T(8,128)(2,1)}, bf16[2,128,896]{2,1,0:T(8,128)(2,1)}, u32[]{:S(2)}, u32[]{:S(2)}) collective-permute-start(bf16[2,128,896]{2,1,0:T(8,128)(2,1)} %collective-permute-done.e01), channel_id=1, source_target_pairs={{0,2},{2,4},{4,6},{6,0},{1,3},{3,5},{5,7},{7,1},{8,10},{10,12},{12... | collective-permute-start | bytes 1376264 | tf_op jit(solution)/shard_map/ppermute | solution.py:370
  28.8 1.2 %copy-start.3 = (bf16[896,896]{1,0:T(8,128)(2,1)}, bf16[896,896]{1,0:T(8,128)(2,1)S(1)}, u32[]{:S(2)}) copy-start(bf16[896,896]{1,0:T(8,128)(2,1)S(1)} %get-tuple-element.121.wq) | copy-start | bytes 4816900
  29.9 1.2 %copy-start.5 = (bf16[896,896]{1,0:T(8,128)(2,1)}, bf16[896,896]{1,0:T(8,128)(2,1)S(1)}, u32[]{:S(2)}) copy-start(bf16[896,896]{1,0:T(8,128)(2,1)S(1)} %get-tuple-element.118.wo) | copy-start | bytes 4816900
  31.1 20.4 %copy-start.9 = (bf16[256,512]{1,0:T(8,128)(2,1)S(1)}, bf16[256,512]{1,0:T(8,128)(2,1)}, u32[]{:S(2)}) copy-start(bf16[256,512]{1,0:T(8,128)(2,1)} %rest_4_.1) | copy-start | bytes 786436
  31.1 20.4 %copy-start.12 = (bf16[2,128,896]{2,1,0:T(8,128)(2,1)S(1)}, bf16[2,128,896]{2,1,0:T(8,128)(2,1)}, u32[]{:S(2)}) copy-start(bf16[2,128,896]{2,1,0:T(8,128)(2,1)} %get-tuple-element.62.e00) | copy-start | bytes 1376260
  31.1 20.4 %copy-start.19 = (s32[4,2]{0,1:T(2,128)S(1)}, s32[4,2]{0,1:T(2,128)}, u32[]{:S(2)}) copy-start(s32[4,2]{0,1:T(2,128)} %param.22) | copy-start | bytes 100
  40.2 11.3 %collective-permute-start.5 = (bf16[2,128,896]{2,1,0:T(8,128)(2,1)}, bf16[2,128,896]{2,1,0:T(8,128)(2,1)S(1)}, u32[]{:S(2)}, u32[]{:S(2)}) collective-permute-start(bf16[2,128,896]{2,1,0:T(8,128)(2,1)} %collective-permute-done.1.e30), channel_id=1, source_target_pairs={{0,2},{2,4},{4,6},{6,0},{1,3},{3,5},{5,7},{7,1},{8,10},{10,12},{12... | collective-permute-start | bytes 1376264 | tf_op jit(solution)/shard_map/ppermute | solution.py:391
  40.2 11.3 %collective-permute-start.6 = (bf16[2,128,896]{2,1,0:T(8,128)(2,1)}, bf16[2,128,896]{2,1,0:T(8,128)(2,1)S(1)}, u32[]{:S(2)}, u32[]{:S(2)}) collective-permute-start(bf16[2,128,896]{2,1,0:T(8,128)(2,1)} %collective-permute-done.3.e11), channel_id=1, source_target_pairs={{0,6},{2,0},{4,2},{6,4},{1,7},{3,1},{5,3},{7,5},{8,14},{10,8},{12,... | collective-permute-start | bytes 1376264 | tf_op jit(solution)/shard_map/ppermute | solution.py:392
  43.4 19.9 %collective-permute-start.10 = (bf16[4,2,256,128]{3,2,1,0:T(8,128)(2,1)S(1)}, bf16[4,2,256,128]{3,2,1,0:T(8,128)(2,1)S(1)}, u32[]{:S(2)}, u32[]{:S(2)}) collective-permute-start(bf16[4,2,256,128]{3,2,1,0:T(8,128)(2,1)S(1)} %slice.4.kv0), channel_id=1, source_target_pairs={{0,16},{16,0},{1,17},{17,1},{2,18},{18,2},{3,19},{19,3},{4,20},{20... | collective-permute-start | bytes 1572872 | tf_op jit(solution)/shard_map/ppermute | solution.py:387
  44.1 19.5 %collective-permute-start.11 = (bf16[4,2,256,128]{3,2,1,0:T(8,128)(2,1)S(1)}, bf16[4,2,256,128]{3,2,1,0:T(8,128)(2,1)S(1)}, u32[]{:S(2)}, u32[]{:S(2)}) collective-permute-start(bf16[4,2,256,128]{3,2,1,0:T(8,128)(2,1)S(1)} %slice.4.kv0), channel_id=1, source_target_pairs={{0,24},{8,16},{16,8},{24,0},{1,25},{9,17},{17,9},{25,1},{2,26},{10... | collective-permute-start | bytes 1572872 | tf_op jit(solution)/shard_map/ppermute | solution.py:388
  44.1 19.5 %collective-permute-start.9 = (bf16[4,2,256,128]{3,2,1,0:T(8,128)(2,1)S(1)}, bf16[4,2,256,128]{3,2,1,0:T(8,128)(2,1)S(1)}, u32[]{:S(2)}, u32[]{:S(2)}) collective-permute-start(bf16[4,2,256,128]{3,2,1,0:T(8,128)(2,1)S(1)} %slice.4.kv0), channel_id=1, source_target_pairs={{0,8},{8,0},{1,9},{9,1},{2,10},{10,2},{3,11},{11,3},{4,12},{12,4},... | collective-permute-start | bytes 1572872 | tf_op jit(solution)/shard_map/ppermute | solution.py:386
  45.6 1.0 copy-start.8
  46.5 1.2 %copy-start.10 = (bf16[896,512]{1,0:T(8,128)(2,1)S(1)}, bf16[896,512]{1,0:T(8,128)(2,1)}, u32[]{:S(2)}) copy-start(bf16[896,512]{1,0:T(8,128)(2,1)} %kw) | copy-start | bytes 2752516
  47.7 1.2 %copy-start.11 = (bf16[896,512]{1,0:T(8,128)(2,1)S(1)}, bf16[896,512]{1,0:T(8,128)(2,1)}, u32[]{:S(2)}) copy-start(bf16[896,512]{1,0:T(8,128)(2,1)} %vw) | copy-start | bytes 2752516
  60.3 11.1 %collective-permute-start.7 = (bf16[2,128,896]{2,1,0:T(8,128)(2,1)S(1)}, bf16[2,128,896]{2,1,0:T(8,128)(2,1)S(1)}, u32[]{:S(2)}, u32[]{:S(2)}) collective-permute-start(bf16[2,128,896]{2,1,0:T(8,128)(2,1)S(1)} %get-tuple-element.86), channel_id=1, source_target_pairs={{0,6},{2,0},{4,2},{6,4},{1,7},{3,1},{5,3},{7,5},{8,14},{10,8},{12,... | collective-permute-start | bytes 1376264 | tf_op jit(solution)/shard_map/ppermute | solution.py:437
  63.4 9.7 %collective-permute-start.8 = (bf16[2,128,896]{2,1,0:T(8,128)(2,1)S(1)}, bf16[2,128,896]{2,1,0:T(8,128)(2,1)S(1)}, u32[]{:S(2)}, u32[]{:S(2)}) collective-permute-start(bf16[2,128,896]{2,1,0:T(8,128)(2,1)S(1)} %get-tuple-element.87), channel_id=1, source_target_pairs={{0,2},{2,4},{4,6},{6,0},{1,3},{3,5},{5,7},{7,1},{8,10},{10,12},{12... | collective-permute-start | bytes 1376264 | tf_op jit(solution)/shard_map/ppermute | solution.py:438
  73.2 11.8 %collective-permute-start.12 = (bf16[2,128,896]{2,1,0:T(8,128)(2,1)S(1)}, bf16[2,128,896]{2,1,0:T(8,128)(2,1)S(1)}, u32[]{:S(2)}, u32[]{:S(2)}) collective-permute-start(bf16[2,128,896]{2,1,0:T(8,128)(2,1)S(1)} %add_convert_fusion.2), channel_id=1, source_target_pairs={{0,6},{2,0},{4,2},{6,4},{1,7},{3,1},{5,3},{7,5},{8,14},{10,8},{12,... | collective-permute-start | bytes 1376264 | tf_op jit(solution)/shard_map/ppermute | solution.py:452
  73.7 12.8 %collective-permute-start.13 = (bf16[2,128,896]{2,1,0:T(8,128)(2,1)S(1)}, bf16[2,128,896]{2,1,0:T(8,128)(2,1)S(1)}, u32[]{:S(2)}, u32[]{:S(2)}) collective-permute-start(bf16[2,128,896]{2,1,0:T(8,128)(2,1)S(1)} %get-tuple-element.100), channel_id=1, source_target_pairs={{0,2},{2,4},{4,6},{6,0},{1,3},{3,5},{5,7},{7,1},{8,10},{10,12},{12... | collective-permute-start | bytes 1376264 | tf_op jit(solution)/shard_map/ppermute | solution.py:453
  75.3 4.8 %collective-permute-start.14 = (bf16[256,128]{1,0:T(8,128)(2,1)S(1)}, bf16[256,128]{1,0:T(8,128)(2,1)S(1)}, u32[]{:S(2)}, u32[]{:S(2)}) collective-permute-start(bf16[256,128]{1,0:T(8,128)(2,1)S(1)} %get-tuple-element.105), channel_id=1, source_target_pairs={{0,96},{32,0},{64,32},{96,64},{1,97},{33,1},{65,33},{97,65},{2,98}... | collective-permute-start | bytes 196616 | tf_op jit(solution)/shard_map/ppermute | solution.py:451
  78.0 5.8 %collective-permute-start.15 = (bf16[256,128]{1,0:T(8,128)(2,1)S(1)}, bf16[256,128]{1,0:T(8,128)(2,1)S(1)}, u32[]{:S(2)}, u32[]{:S(2)}) collective-permute-start(bf16[256,128]{1,0:T(8,128)(2,1)S(1)} %get-tuple-element.106), channel_id=1, source_target_pairs={{0,64},{32,96},{64,0},{96,32},{1,65},{33,97},{65,1},{97,33},{2,66}... | collective-permute-start | bytes 196616 | tf_op jit(solution)/shard_map/ppermute | solution.py:451
  78.9 5.6 %collective-permute-start.16 = (bf16[256,128]{1,0:T(8,128)(2,1)S(1)}, bf16[256,128]{1,0:T(8,128)(2,1)S(1)}, u32[]{:S(2)}, u32[]{:S(2)}) collective-permute-start(bf16[256,128]{1,0:T(8,128)(2,1)S(1)} %get-tuple-element.107), channel_id=1, source_target_pairs={{0,32},{32,64},{64,96},{96,0},{1,33},{33,65},{65,97},{97,1},{2,34}... | collective-permute-start | bytes 196616 | tf_op jit(solution)/shard_map/ppermute | solution.py:451
  79.7 19.8 %copy-start.6 = (bf16[896,896]{1,0:T(8,128)(2,1)S(1)}, bf16[896,896]{1,0:T(8,128)(2,1)}, u32[]{:S(2)}) copy-start(bf16[896,896]{1,0:T(8,128)(2,1)} %copy-done.5) | copy-start | bytes 4816900
  79.8 19.7 %copy-start.4 = (bf16[896,896]{1,0:T(8,128)(2,1)S(1)}, bf16[896,896]{1,0:T(8,128)(2,1)}, u32[]{:S(2)}) copy-start(bf16[896,896]{1,0:T(8,128)(2,1)} %copy-done.3) | copy-start | bytes 4816900
  79.8 19.6 %copy-start.13 = (f32[2,256,128]{2,1,0:T(8,128)S(1)}, f32[2,256,128]{2,1,0:T(8,128)}, u32[]{:S(2)}) copy-start(f32[2,256,128]{2,1,0:T(8,128)} %get-tuple-element.63.wt) | copy-start | bytes 786436
  79.8 19.6 %copy-start.17 = (bf16[2,64,896]{2,1,0:T(8,128)(2,1)S(1)}, bf16[2,64,896]{2,1,0:T(8,128)(2,1)}, u32[]{:S(2)}) copy-start(bf16[2,64,896]{2,1,0:T(8,128)(2,1)} %get-tuple-element.120.ek) | copy-start | bytes 688132
  79.8 19.6 %copy-start.18 = (bf16[2,64,896]{2,1,0:T(8,128)(2,1)S(1)}, bf16[2,64,896]{2,1,0:T(8,128)(2,1)}, u32[]{:S(2)}) copy-start(bf16[2,64,896]{2,1,0:T(8,128)(2,1)} %get-tuple-element.119.ev) | copy-start | bytes 688132
  86.6 12.3 %collective-permute-start.19 = (bf16[2,128,896]{2,1,0:T(8,128)(2,1)S(1)}, bf16[2,128,896]{2,1,0:T(8,128)(2,1)S(1)}, u32[]{:S(2)}, u32[]{:S(2)}) collective-permute-start(bf16[2,128,896]{2,1,0:T(8,128)(2,1)S(1)} %add_convert_fusion), channel_id=1, source_target_pairs={{0,1},{1,0},{2,3},{3,2},{4,5},{5,4},{6,7},{7,6},{8,9},{9,8},{10,11... | collective-permute-start | bytes 1376264 | tf_op jit(solution)/shard_map/ppermute | solution.py:457
  87.9 11.5 %collective-permute-start.17 = (bf16[2,128,896]{2,1,0:T(8,128)(2,1)S(1)}, bf16[2,128,896]{2,1,0:T(8,128)(2,1)S(1)}, u32[]{:S(2)}, u32[]{:S(2)}) collective-permute-start(bf16[2,128,896]{2,1,0:T(8,128)(2,1)S(1)} %add_convert_fusion.1), channel_id=1, source_target_pairs={{0,2},{2,4},{4,6},{6,0},{1,3},{3,5},{5,7},{7,1},{8,10},{10,12},{12... | collective-permute-start | bytes 1376264 | tf_op jit(solution)/shard_map/ppermute | solution.py:458
  88.2 11.2 %collective-permute-start.18 = (bf16[2,128,896]{2,1,0:T(8,128)(2,1)S(1)}, bf16[2,128,896]{2,1,0:T(8,128)(2,1)S(1)}, u32[]{:S(2)}, u32[]{:S(2)}) collective-permute-start(bf16[2,128,896]{2,1,0:T(8,128)(2,1)S(1)} %get-tuple-element.114), channel_id=1, source_target_pairs={{0,6},{2,0},{4,2},{6,4},{1,7},{3,1},{5,3},{7,5},{8,14},{10,8},{12,... | collective-permute-start | bytes 1376264 | tf_op jit(solution)/shard_map/ppermute | solution.py:459

commit v2 on v1

--- a/solution.py
+++ b/solution.py
@@ -222,10 +222,13 @@
     return jnp.concatenate(parts, axis=0)
 
 
-def cross_kernel(ids, e00, e01, e10, e11, e20, e21, e30, e31, *rest):
-    blocks = (e00, e01, e10, e11, e20, e21, e30, e31)
+def cross_kernel(ids, e00, e01, e10, e11, e21, e30, up, *rest):
+    slots = e00.shape[0]
+    blocks = (e00, e01, e10, e11, up.at[slots:], e21, e30, up.at[:slots])
     kvw, qm_t, gm_t, q, g, kv_t, cross = rest[:7]
-    outs, (table, held, sent, ckv, dkv) = rest[7:15], rest[15:]
+    p00, p01, p10, far, p21, p30, p31 = rest[7:14]
+    outs = (p00, p01, p10, far.at[slots:], far.at[:slots], p21, p30, p31)
+    table, held, sent, ckv, dkv = rest[14:]
     width = q.shape[1]
     z, yh = lax.axis_index("z"), lax.axis_index("yh")
     n_named = held.shape[0]
@@ -249,7 +252,7 @@
 
         @pl.when(n < 0)
         def _():
-            outs[i][t] = jnp.zeros(outs[i].shape[1:], BF16)
+            outs[i][t] = jnp.zeros((NL, e00.shape[2]), BF16)
 
     heads = width // HSIZE
     pair = 2 * NL
@@ -367,7 +370,7 @@
 
     e01, e30, e10, packed = after((e01, e30, e10, packed))
     e11 = lax.ppermute(e01, "z", shift(NX, -1))
-    e31 = lax.ppermute(e01, "z", shift(NX, 1))
+    up = lax.ppermute(jnp.concatenate([e01, e30]), "z", shift(NX, 1))
 
 
     weights = after((enc_q, enc_o, e01))[:2]
@@ -379,7 +382,7 @@
     )(*weights)
 
     own_kv = pieces[:, 1:]
-    e30, e11, e31, own_kv, *turned = after((e30, e11, e31, own_kv, *turned))
+    e11, own_kv, *turned = after((e11, own_kv, *turned))
     swap = [(0, 3), (1, 2), (2, 1), (3, 0)]
     kvs = [
         own_kv,
@@ -388,7 +391,6 @@
         lax.ppermute(own_kv, ("yl", "core"), swap),
     ]
     wq_t, wo_t = turned
-    e20 = lax.ppermute(e30, "z", shift(NX, 1))
     e21 = lax.ppermute(e11, "z", shift(NX, -1))
 
     given = after((cross_k_weight, cross_v_weight, cross_q, mixed_grad, e11))[:4]
@@ -402,9 +404,10 @@
 
     cross, *p = call(
         cross_kernel,
-        out_shape=[struct((rows, width), F32)] + [struct((slots, nl, ew), BF16)] * 8,
-        in_specs=[smem()] + [vmem()] * 14,
-        out_specs=[vmem()] * 9,
+        out_shape=[struct((rows, width), F32)]
+        + [struct((k * slots, nl, ew), BF16) for k in (1, 1, 1, 2, 1, 1, 1)],
+        in_specs=[smem()] + [vmem()] * 13,
+        out_specs=[vmem()] * 8,
         scratch_shapes=[
             pltpu.SMEM((16,), jnp.int32),
             pltpu.VMEM((n_named, nl, ew), BF16),
@@ -418,10 +421,9 @@
         e01,
         e10,
         e11,
-        e20,
         e21,
         e30,
-        e31,
+        up,
         kvw,
         qm_t,
         gm_t,
@@ -429,13 +431,13 @@
         mixed_grad,
         kv_t,
     )
-    p00, p01, p10, p11, p20, p21, p30, p31 = p
+    p00, p01, p10, far, p21, p30, p31 = p
 
     def add(a, b):
         return (a.astype(F32) + b.astype(F32)).astype(BF16)
 
     far1 = lax.ppermute(p21, "z", shift(NX, -1))
-    far0 = lax.ppermute(p20, "z", shift(NX, 1))
+    far = lax.ppermute(far, "z", shift(NX, 1))
     *kvs, _ = after((*kvs, cross))
     outs = call(
         attend_kernel,
@@ -447,12 +449,11 @@
             pltpu.VMEM((rows, 1), F32),
         ],
     )(pieces, *kvs)
-    far1, far0, p11, *outs = after((far1, far0, p11, *outs))
+    far1, *outs = after((far1, *outs))
     selfs = [outs[0]] + [lax.ppermute(outs[d], "x", shift(NX, -d)) for d in range(1, NX)]
     down1 = lax.ppermute(add(p31, far1), "z", shift(NX, -1))
-    up1 = lax.ppermute(p11, "z", shift(NX, 1))
-    near0 = add(p10, far0)
-    down1, up1, near0, p30, *selfs = after((down1, up1, near0, p30, *selfs))
+    down1, far, p30, *selfs = after((down1, far, p30, *selfs))
+    near0, up1 = add(p10, far[:slots]), far[slots:]
     theirs = (p01.astype(F32) + up1.astype(F32) + down1.astype(F32)).astype(BF16)
     other = lax.ppermute(theirs, "yh", shift(2, 1))
     up0 = lax.ppermute(near0, "z", shift(NX, 1))

time: 103 us -> 103 us (level)
  starting transfers between devices: 34 us -> 31.5 us
  other arithmetic: 0.39 us -> 2.56 us
    ppermute x1, waiting for transfers between devices: 0.51 us -> 8.43 us  [local(): up0 = lax.ppermute(near0, 'z', shift(NX, 1))]
    ppermute x1, waiting for transfers between devices: 6.94 us -> 0.39 us  [local(): other = lax.ppermute(theirs, 'yh', shift(2, 1))]
    ppermute x4 -> x2, waiting for transfers between devices: 8.02 us -> 3.76 us  [the longest x1 3.75 us: local(): up = lax.ppermute(jnp.concatenate([e01, e30]), 'z', shift(NX, 1))]
    ppermute x1, starting transfers between devices: 3.03 us -> 0.08 us  [local(): far1 = lax.ppermute(p21, 'z', shift(NX, -1))]
    ppermute x1, waiting for transfers between devices: 0.53 us -> 2.73 us  [local(): down1 = lax.ppermute(add(p31, far1), 'z', shift(NX, -1))]
    ppermute x1, waiting for transfers between devices: 0.2 us -> 2.38 us  [local(): lax.ppermute(own_kv, ('yl', 'core'), swap)]
    concatenate x0 -> x1, other arithmetic: none -> 2.17 us  [local(): up = lax.ppermute(jnp.concatenate([e01, e30]), 'z', shift(NX, 1))]
    ppermute x1, waiting for transfers between devices: 4.01 us -> 2.3 us  [local(): e11 = lax.ppermute(e01, 'z', shift(NX, -1))]
  transfers between devices with their start and end apart: 21 -> 19, of which waited for: 16 -> 12; matrix products, arithmetic and copies ran while one was open for 1% -> 3% of each run, Pallas kernels for 18% -> 18%
where the time goes in v2:
time: 103 us
  waiting for transfers between devices  32.1 us (31%)
  starting transfers between devices  31.5 us (31%)
  Pallas kernels  27.8 us (27%)
  local copies, waits for them, and re-layouts  7.73 us (8%)
  other arithmetic  2.56 us (2%)
    pallas_call x1, Pallas kernels, local(): call(cross_kernel, out_shape=[struct((rows, width), F32)] + [struct((k *...  8.96 us
    ppermute x1, waiting for transfers between devices, local(): up0 = lax.ppermute(near0, 'z', shift(NX, 1))  8.43 us
    pallas_call x1, Pallas kernels, local(): call(attend_kernel, out_shape=[struct((rows, HSIZE), BF16)] * NX, in_spec...  6.82 us
    unnamed x40, local copies, waits for them, and re-layouts  6.58 us
    pallas_call x1, Pallas kernels, local(): call(encode_kernel, mib=56, out_shape=[struct((slots, nl, ew), BF16), str...  6.25 us
    ppermute x3, waiting for transfers between devices, local(): lax.ppermute(outs[d], 'x', shift(NX, -d))  5.44 us
    ppermute x3, starting transfers between devices, local(): lax.ppermute(outs[d], 'x', shift(NX, -d))  4.65 us
    all_to_all x1, starting transfers between devices, local(): pieces = lax.all_to_all(packed, 'x', 0, 0)  4.54 us
  transfers between devices with their start and end apart: 19, of which 12 were waited for; matrix products, arithmetic and copies ran while one was open for 3% of the time, Pallas kernels for 18%

profile of v2, /device:TPU:0, one launch (start us, length us, event | category | flops | bytes accessed | tf_op | source)
XLA Modules:
  0.0 102.6 jit_solution(5835650755195741121)
XLA Ops:
  0.6 0.0 copy-start.14
  0.6 0.0 copy-start.15
  0.7 0.0 copy-start.16
  0.7 6.2 %shard_map.149 = (bf16[2,128,896]{2,1,0:T(8,128)(2,1)}, f32[2,256,128]{2,1,0:T(8,128)}, bf16[2,64,896]{2,1,0:T(8,128)(2,1)}, bf16[2,64,896]{2,1,0:T(8,128)(2,1)}) custom-call(s32[2,4]{1,0:T(2,128)} %bitcast.1, bf16[2,128,896]{2,1,0:T(8,128)(2,1)} %nb_h.1, bf16[256,896]{1,0:T(8,128)(2,1)} %ctx_h.1, bf16[896,896]{1,0:T(8,128)(2,1)} %wq, ...), custom_call_target="tpu_custom_call" | custom-call | tf_op jit(solution)/shard_map/pallas_call | solution.py:342
  6.9 3.4 %collective-permute-start = (bf16[2,128,896]{2,1,0:T(8,128)(2,1)}, bf16[2,128,896]{2,1,0:T(8,128)(2,1)}, u32[]{:S(2)}, u32[]{:S(2)}) collective-permute-start(bf16[2,128,896]{2,1,0:T(8,128)(2,1)} %get-tuple-element.56.e00), channel_id=1, source_target_pairs={{0,1},{1,0},{2,3},{3,2},{4,5},{5,4},{6,7},{7,6},{8,9},{9,8},{10,11... | collective-permute-start | bytes 1376264 | tf_op jit(solution)/shard_map/ppermute | solution.py:358
  10.3 1.9 %collective-permute-start.1 = (bf16[2,128,896]{2,1,0:T(8,128)(2,1)}, bf16[2,128,896]{2,1,0:T(8,128)(2,1)}, u32[]{:S(2)}, u32[]{:S(2)}) collective-permute-start(bf16[2,128,896]{2,1,0:T(8,128)(2,1)} %get-tuple-element.56.e00), channel_id=1, source_target_pairs={{0,2},{2,4},{4,6},{6,0},{1,3},{3,5},{5,7},{7,1},{8,10},{10,12},{12... | collective-permute-start | bytes 1376264 | tf_op jit(solution)/shard_map/ppermute | solution.py:359
  12.2 2.1 %collective-permute-start.2 = (bf16[2,128,896]{2,1,0:T(8,128)(2,1)}, bf16[2,128,896]{2,1,0:T(8,128)(2,1)}, u32[]{:S(2)}, u32[]{:S(2)}) collective-permute-start(bf16[2,128,896]{2,1,0:T(8,128)(2,1)} %get-tuple-element.56.e00), channel_id=1, source_target_pairs={{0,6},{2,0},{4,2},{6,4},{1,7},{3,1},{5,3},{7,5},{8,14},{10,8},{12,... | collective-permute-start | bytes 1376264 | tf_op jit(solution)/shard_map/ppermute | solution.py:360
  14.3 0.0 copy-done.14
  14.3 0.0 copy-done.16
  14.3 0.1 shard_map.150
  14.5 0.9 copy-done.2
  15.4 4.5 %all-to-all-start = ((bf16[4,3,256,128]{3,2,1,0:T(8,128)(2,1)}), bf16[4,3,256,128]{3,2,1,0:T(8,128)(2,1)}, u32[]{:S(2)}, u32[]{:S(2)}) async-start(bf16[4,3,256,128]{3,2,1,0:T(8,128)(2,1)} %copy-done.2), calls=%async_computation | async-start | bytes 1572864 | tf_op jit(solution)/shard_map/all_to_all | solution.py:369
  19.9 1.2 %collective-permute-done.e01 = bf16[2,128,896]{2,1,0:T(8,128)(2,1)} collective-permute-done((bf16[2,128,896]{2,1,0:T(8,128)(2,1)}, bf16[2,128,896]{2,1,0:T(8,128)(2,1)}, u32[]{:S(2)}, u32[]{:S(2)}) %collective-permute-start) | collective-permute-done | bytes 458784 | tf_op jit(solution)/shard_map/ppermute | solution.py:358
  21.1 3.8 %collective-permute-done.1.e30 = bf16[2,128,896]{2,1,0:T(8,128)(2,1)} collective-permute-done((bf16[2,128,896]{2,1,0:T(8,128)(2,1)}, bf16[2,128,896]{2,1,0:T(8,128)(2,1)}, u32[]{:S(2)}, u32[]{:S(2)}) %collective-permute-start.1) | collective-permute-done | bytes 458784 | tf_op jit(solution)/shard_map/ppermute | solution.py:359
  24.9 0.0 collective-permute-done.2.e10
  24.9 2.9 %collective-permute-start.3 = (bf16[2,128,896]{2,1,0:T(8,128)(2,1)}, bf16[2,128,896]{2,1,0:T(8,128)(2,1)}, u32[]{:S(2)}, u32[]{:S(2)}) collective-permute-start(bf16[2,128,896]{2,1,0:T(8,128)(2,1)} %collective-permute-done.e01), channel_id=1, source_target_pairs={{0,6},{2,0},{4,2},{6,4},{1,7},{3,1},{5,3},{7,5},{8,14},{10,8},{12,... | collective-permute-start | bytes 1376264 | tf_op jit(solution)/shard_map/ppermute | solution.py:372
  27.8 2.2 %pad_maximum_fusion = bf16[4,128,896]{2,1,0:T(8,128)(2,1)} fusion(bf16[2,128,896]{2,1,0:T(8,128)(2,1)} %collective-permute-done.1.e30, bf16[2,128,896]{2,1,0:T(8,128)(2,1)} %collective-permute-done.e01), kind=kLoop, calls=%fused_computation | loop fusion | flops 458752 | bytes 1835008 | tf_op jit(solution)/shard_map/concatenate | solution.py:373
  30.0 0.0 collective-permute-start.5
  30.0 0.0 copy-done
  30.0 0.0 copy-done.1
  30.0 0.9 shard_map.151
  30.9 1.2 %copy-done.3 = bf16[896,896]{1,0:T(8,128)(2,1)} copy-done((bf16[896,896]{1,0:T(8,128)(2,1)}, bf16[896,896]{1,0:T(8,128)(2,1)S(1)}, u32[]{:S(2)}) %copy-start.3) | copy-done | bytes 1605656
  32.1 1.2 %copy-done.5 = bf16[896,896]{1,0:T(8,128)(2,1)} copy-done((bf16[896,896]{1,0:T(8,128)(2,1)}, bf16[896,896]{1,0:T(8,128)(2,1)S(1)}, u32[]{:S(2)}) %copy-start.5) | copy-done | bytes 1605656
  33.3 0.0 all-to-all-done.pieces
  33.3 1.1 %slice.12.kv0 = bf16[4,2,256,128]{3,2,1,0:T(8,128)(2,1)S(1)} slice(bf16[4,3,256,128]{3,2,1,0:T(8,128)(2,1)} %all-to-all-done.pieces), slice={[0:4], [1:3], [0:256], [0:128]} | slice | bytes 1048576 | tf_op jit(solution)/shard_map/slice | solution.py:384
  34.4 2.3 %collective-permute-done.3.e11 = bf16[2,128,896]{2,1,0:T(8,128)(2,1)} collective-permute-done((bf16[2,128,896]{2,1,0:T(8,128)(2,1)}, bf16[2,128,896]{2,1,0:T(8,128)(2,1)}, u32[]{:S(2)}, u32[]{:S(2)}) %collective-permute-start.3) | collective-permute-done | bytes 458784 | tf_op jit(solution)/shard_map/ppermute | solution.py:372
  36.7 3.7 %collective-permute-start.4 = (bf16[2,128,896]{2,1,0:T(8,128)(2,1)}, bf16[2,128,896]{2,1,0:T(8,128)(2,1)S(1)}, u32[]{:S(2)}, u32[]{:S(2)}) collective-permute-start(bf16[2,128,896]{2,1,0:T(8,128)(2,1)} %collective-permute-done.3.e11), channel_id=1, source_target_pairs={{0,6},{2,0},{4,2},{6,4},{1,7},{3,1},{5,3},{7,5},{8,14},{10,8},{12,... | collective-permute-start | bytes 1376264 | tf_op jit(solution)/shard_map/ppermute | solution.py:394
  40.4 0.0 collective-permute-start.7
  40.4 0.7 collective-permute-start.8
  41.1 1.2 %collective-permute-start.9 = (bf16[4,2,256,128]{3,2,1,0:T(8,128)(2,1)S(1)}, bf16[4,2,256,128]{3,2,1,0:T(8,128)(2,1)S(1)}, u32[]{:S(2)}, u32[]{:S(2)}) collective-permute-start(bf16[4,2,256,128]{3,2,1,0:T(8,128)(2,1)S(1)} %slice.12.kv0), channel_id=1, source_target_pairs={{0,24},{8,16},{16,8},{24,0},{1,25},{9,17},{17,9},{25,1},{2,26},{10... | collective-permute-start | bytes 1572872 | tf_op jit(solution)/shard_map/ppermute | solution.py:391
  42.3 0.9 copy-done.8
  43.2 1.2 %copy-done.10 = bf16[896,512]{1,0:T(8,128)(2,1)S(1)} copy-done((bf16[896,512]{1,0:T(8,128)(2,1)S(1)}, bf16[896,512]{1,0:T(8,128)(2,1)}, u32[]{:S(2)}) %copy-start.10) | copy-done | bytes 917528
  44.4 1.2 %copy-done.11 = bf16[896,512]{1,0:T(8,128)(2,1)S(1)} copy-done((bf16[896,512]{1,0:T(8,128)(2,1)S(1)}, bf16[896,512]{1,0:T(8,128)(2,1)}, u32[]{:S(2)}) %copy-start.11) | copy-done | bytes 917528
  45.6 1.1 %shard_map.152 = (bf16[896,1024]{1,0:T(8,128)(2,1)S(1)}, bf16[1024,896]{1,0:T(8,128)(2,1)S(1)}, bf16[4,512,256]{2,1,0:T(8,128)(2,1)S(1)}, bf16[4,512,256]{2,1,0:T(8,128)(2,1)S(1)}) custom-call(bf16[896,512]{1,0:T(8,128)(2,1)S(1)} %copy-done.10, bf16[896,512]{1,0:T(8,128)(2,1)S(1)} %copy-done.11, bf16[256,512]{1,0:T(8,128)(2,1)S(1)} %copy-done.7, ...), custom_call_target="tpu_custom_call" | custom-call | tf_op jit(solution)/shard_map/pallas_call | solution.py:397
  46.7 1.6 %collective-permute-done.4.e21 = bf16[2,128,896]{2,1,0:T(8,128)(2,1)S(1)} collective-permute-done((bf16[2,128,896]{2,1,0:T(8,128)(2,1)}, bf16[2,128,896]{2,1,0:T(8,128)(2,1)S(1)}, u32[]{:S(2)}, u32[]{:S(2)}) %collective-permute-start.4) | collective-permute-done | bytes 458784 | tf_op jit(solution)/shard_map/ppermute | solution.py:394
  48.4 3.8 %collective-permute-done.5.up = bf16[4,128,896]{2,1,0:T(8,128)(2,1)} collective-permute-done((bf16[4,128,896]{2,1,0:T(8,128)(2,1)}, bf16[4,128,896]{2,1,0:T(8,128)(2,1)}, u32[]{:S(2)}, u32[]{:S(2)}) %collective-permute-start.5) | collective-permute-done | bytes 917536 | tf_op jit(solution)/shard_map/ppermute | solution.py:373
  52.1 0.0 copy-done.19
  52.1 9.0 %shard_map.153 = (f32[256,512]{1,0:T(8,128)S(1)}, bf16[2,128,896]{2,1,0:T(8,128)(2,1)S(1)}, bf16[2,128,896]{2,1,0:T(8,128)(2,1)S(1)}, bf16[2,128,896]{2,1,0:T(8,...) custom-call(s32[2,4]{1,0:T(2,128)S(1)} %bitcast.2, ...), custom_call_target="tpu_custom_call" | custom-call | tf_op jit(solution)/shard_map/pallas_call | solution.py:405
  61.1 0.1 collective-permute-start.6
  61.2 2.0 %collective-permute-start.11 = (bf16[4,128,896]{2,1,0:T(8,128)(2,1)S(1)}, bf16[4,128,896]{2,1,0:T(8,128)(2,1)S(1)}, u32[]{:S(2)}, u32[]{:S(2)}) collective-permute-start(bf16[4,128,896]{2,1,0:T(8,128)(2,1)S(1)} %get-tuple-element.90), channel_id=1, source_target_pairs={{0,2},{2,4},{4,6},{6,0},{1,3},{3,5},{5,7},{7,1},{8,10},{10,12},{12... | collective-permute-start | bytes 2752520 | tf_op jit(solution)/shard_map/ppermute | solution.py:440
  63.2 0.0 collective-permute-done.7.kv1
  63.2 0.0 collective-permute-done.8.kv2
  63.2 2.4 %collective-permute-done.9.kv3 = bf16[4,2,256,128]{3,2,1,0:T(8,128)(2,1)S(1)} collective-permute-done((bf16[4,2,256,128]{3,2,1,0:T(8,128)(2,1)S(1)}, bf16[4,2,256,128]{3,2,1,0:T(8,128)(2,1)S(1)}, u32[]{:S(2)}, u32[]{:S(2)}) %collective-permute-start.9) | collective-permute-done | bytes 524320 | tf_op jit(solution)/shard_map/ppermute | solution.py:391
  65.6 6.8 %shard_map.154 = (bf16[256,128]{1,0:T(8,128)(2,1)S(1)}, bf16[256,128]{1,0:T(8,128)(2,1)S(1)}, bf16[256,128]{1,0:T(8,128)(2,1)S(1)}, bf16[256,128]{1,0:T(8,128)(2,1)S(1)}) custom-call(bf16[4,3,256,128]{3,2,1,0:T(8,128)(2,1)} %all-to-all-done.pieces, bf16[4,2,256,128]{3,2,1,0:T(8,128)(2,1)S(1)} %slice.12.kv0, ...), custom_call_target="tpu_custom_call" | custom-call | tf_op jit(solution)/shard_map/pallas_call | solution.py:442
  72.4 0.0 collective-permute-done.6
  72.4 0.1 add_convert_fusion.2
  72.5 0.2 collective-permute-start.10
  72.7 3.0 %collective-permute-start.12 = (bf16[256,128]{1,0:T(8,128)(2,1)S(1)}, bf16[256,128]{1,0:T(8,128)(2,1)S(1)}, u32[]{:S(2)}, u32[]{:S(2)}) collective-permute-start(bf16[256,128]{1,0:T(8,128)(2,1)S(1)} %get-tuple-element.93), channel_id=1, source_target_pairs={{0,96},{32,0},{64,32},{96,64},{1,97},{33,1},{65,33},{97,65},{2,98}... | collective-permute-start | bytes 196616 | tf_op jit(solution)/shard_map/ppermute | solution.py:453
  75.7 0.8 collective-permute-start.13
  76.5 0.9 collective-permute-start.14
  77.4 1.8 %collective-permute-done.12.s1 = bf16[256,128]{1,0:T(8,128)(2,1)S(1)} collective-permute-done((bf16[256,128]{1,0:T(8,128)(2,1)S(1)}, bf16[256,128]{1,0:T(8,128)(2,1)S(1)}, u32[]{:S(2)}, u32[]{:S(2)}) %collective-permute-start.12) | collective-permute-done | bytes 65568 | tf_op jit(solution)/shard_map/ppermute | solution.py:453
  79.1 3.0 %collective-permute-done.13.s2 = bf16[256,128]{1,0:T(8,128)(2,1)S(1)} collective-permute-done((bf16[256,128]{1,0:T(8,128)(2,1)S(1)}, bf16[256,128]{1,0:T(8,128)(2,1)S(1)}, u32[]{:S(2)}, u32[]{:S(2)}) %collective-permute-start.13) | collective-permute-done | bytes 65568 | tf_op jit(solution)/shard_map/ppermute | solution.py:453
  82.1 0.7 collective-permute-done.14.s3
  82.8 2.7 %collective-permute-done.10 = bf16[2,128,896]{2,1,0:T(8,128)(2,1)S(1)} collective-permute-done((bf16[2,128,896]{2,1,0:T(8,128)(2,1)S(1)}, bf16[2,128,896]{2,1,0:T(8,128)(2,1)S(1)}, u32[]{:S(2)}, u32[]{:S(2)}) %collective-permute-start.10) | collective-permute-done | bytes 458784 | tf_op jit(solution)/shard_map/ppermute | solution.py:454
  85.5 0.0 collective-permute-done.11
  85.6 0.3 add_convert_fusion
  85.9 0.1 collective-permute-start.15
  86.0 1.0 collective-permute-start.17
  86.9 3.1 %collective-permute-start.16 = (bf16[2,128,896]{2,1,0:T(8,128)(2,1)S(1)}, bf16[2,128,896]{2,1,0:T(8,128)(2,1)S(1)}, u32[]{:S(2)}, u32[]{:S(2)}) collective-permute-start(bf16[2,128,896]{2,1,0:T(8,128)(2,1)S(1)} %get-tuple-element.103), channel_id=1, source_target_pairs={{0,6},{2,0},{4,2},{6,4},{1,7},{3,1},{5,3},{7,5},{8,14},{10,8},{12,... | collective-permute-start | bytes 1376264 | tf_op jit(solution)/shard_map/ppermute | solution.py:460
  90.1 0.8 shard_map.155
  90.9 8.4 %collective-permute-done.15.d1 = bf16[2,128,896]{2,1,0:T(8,128)(2,1)S(1)} collective-permute-done((bf16[2,128,896]{2,1,0:T(8,128)(2,1)S(1)}, bf16[2,128,896]{2,1,0:T(8,128)(2,1)S(1)}, u32[]{:S(2)}, u32[]{:S(2)}) %collective-permute-start.15) | collective-permute-done | bytes 458784 | tf_op jit(solution)/shard_map/ppermute | solution.py:459
  99.3 0.4 collective-permute-done.17.d3
  99.7 0.0 collective-permute-done.16.d2
  99.7 2.8 %shard_map.156 = f32[2,128,896]{2,1,0:T(8,128)} custom-call(bf16[2,128,896]{2,1,0:T(8,128)(2,1)S(1)} %get-tuple-element.100.d0, bf16[2,128,896]{2,1,0:T(8,128)(2,1)S(1)} %collective-permute-done.15.d1, bf16[2,128,896]{2,1,0:T(8,128)(2,1)S(1)} %collective-permute-done.16.d2, bf16[2,128,896]{2,1,0:T(8,128)(2,1)S(1)} %collective-permute-done.17.d3, ...), custom_call_target="tpu_custom_call" | custom-call | tf_op jit(solution)/shard_map/pallas_call | solution.py:462
  (26 shorter events, 0.0 us)
Async XLA Ops:
  0.6 13.7 %copy-start.14 = (bf16[256,512]{1,0:T(8,128)(2,1)S(1)}, bf16[256,512]{1,0:T(8,128)(2,1)}, u32[]{:S(2)}) copy-start(bf16[256,512]{1,0:T(8,128)(2,1)} %q_ref) | copy-start | bytes 786436
  0.6 13.7 %copy-start.15 = (bf16[256,512]{1,0:T(8,128)(2,1)S(1)}, bf16[256,512]{1,0:T(8,128)(2,1)}, u32[]{:S(2)}) copy-start(bf16[256,512]{1,0:T(8,128)(2,1)} %k_ref) | copy-start | bytes 786436
  0.7 13.7 %copy-start.16 = (bf16[256,512]{1,0:T(8,128)(2,1)S(1)}, bf16[256,512]{1,0:T(8,128)(2,1)}, u32[]{:S(2)}) copy-start(bf16[256,512]{1,0:T(8,128)(2,1)} %v_ref) | copy-start | bytes 786436
  6.9 14.2 %collective-permute-start = (bf16[2,128,896]{2,1,0:T(8,128)(2,1)}, bf16[2,128,896]{2,1,0:T(8,128)(2,1)}, u32[]{:S(2)}, u32[]{:S(2)}) collective-permute-start(bf16[2,128,896]{2,1,0:T(8,128)(2,1)} %get-tuple-element.56.e00), channel_id=1, source_target_pairs={{0,1},{1,0},{2,3},{3,2},{4,5},{5,4},{6,7},{7,6},{8,9},{9,8},{10,11... | collective-permute-start | bytes 1376264 | tf_op jit(solution)/shard_map/ppermute | solution.py:358
  10.3 14.6 %collective-permute-start.1 = (bf16[2,128,896]{2,1,0:T(8,128)(2,1)}, bf16[2,128,896]{2,1,0:T(8,128)(2,1)}, u32[]{:S(2)}, u32[]{:S(2)}) collective-permute-start(bf16[2,128,896]{2,1,0:T(8,128)(2,1)} %get-tuple-element.56.e00), channel_id=1, source_target_pairs={{0,2},{2,4},{4,6},{6,0},{1,3},{3,5},{5,7},{7,1},{8,10},{10,12},{12... | collective-permute-start | bytes 1376264 | tf_op jit(solution)/shard_map/ppermute | solution.py:359
  12.2 12.7 %collective-permute-start.2 = (bf16[2,128,896]{2,1,0:T(8,128)(2,1)}, bf16[2,128,896]{2,1,0:T(8,128)(2,1)}, u32[]{:S(2)}, u32[]{:S(2)}) collective-permute-start(bf16[2,128,896]{2,1,0:T(8,128)(2,1)} %get-tuple-element.56.e00), channel_id=1, source_target_pairs={{0,6},{2,0},{4,2},{6,4},{1,7},{3,1},{5,3},{7,5},{8,14},{10,8},{12,... | collective-permute-start | bytes 1376264 | tf_op jit(solution)/shard_map/ppermute | solution.py:360
  14.5 0.9 copy-start.2
  15.4 14.6 %copy-start = (bf16[896,896]{1,0:T(8,128)(2,1)S(1)}, bf16[896,896]{1,0:T(8,128)(2,1)}, u32[]{:S(2)}) copy-start(bf16[896,896]{1,0:T(8,128)(2,1)} %wq) | copy-start | bytes 4816900
  15.4 14.6 %copy-start.1 = (bf16[896,896]{1,0:T(8,128)(2,1)S(1)}, bf16[896,896]{1,0:T(8,128)(2,1)}, u32[]{:S(2)}) copy-start(bf16[896,896]{1,0:T(8,128)(2,1)} %wo) | copy-start | bytes 4816900
  15.4 17.9 %all-to-all-start = ((bf16[4,3,256,128]{3,2,1,0:T(8,128)(2,1)}), bf16[4,3,256,128]{3,2,1,0:T(8,128)(2,1)}, u32[]{:S(2)}, u32[]{:S(2)}) async-start(bf16[4,3,256,128]{3,2,1,0:T(8,128)(2,1)} %copy-done.2), calls=%async_computation | async-start | bytes 1572864 | tf_op jit(solution)/shard_map/all_to_all | solution.py:369
  24.9 11.8 %collective-permute-start.3 = (bf16[2,128,896]{2,1,0:T(8,128)(2,1)}, bf16[2,128,896]{2,1,0:T(8,128)(2,1)}, u32[]{:S(2)}, u32[]{:S(2)}) collective-permute-start(bf16[2,128,896]{2,1,0:T(8,128)(2,1)} %collective-permute-done.e01), channel_id=1, source_target_pairs={{0,6},{2,0},{4,2},{6,4},{1,7},{3,1},{5,3},{7,5},{8,14},{10,8},{12,... | collective-permute-start | bytes 1376264 | tf_op jit(solution)/shard_map/ppermute | solution.py:372
  30.0 12.3 %copy-start.7 = (bf16[256,512]{1,0:T(8,128)(2,1)S(1)}, bf16[256,512]{1,0:T(8,128)(2,1)}, u32[]{:S(2)}) copy-start(bf16[256,512]{1,0:T(8,128)(2,1)} %rest_3_.1) | copy-start | bytes 786436
  30.0 22.1 %collective-permute-start.5 = (bf16[4,128,896]{2,1,0:T(8,128)(2,1)}, bf16[4,128,896]{2,1,0:T(8,128)(2,1)}, u32[]{:S(2)}, u32[]{:S(2)}) collective-permute-start(bf16[4,128,896]{2,1,0:T(8,128)(2,1)} %pad_maximum_fusion), channel_id=1, source_target_pairs={{0,2},{2,4},{4,6},{6,0},{1,3},{3,5},{5,7},{7,1},{8,10},{10,12},{12... | collective-permute-start | bytes 2752520 | tf_op jit(solution)/shard_map/ppermute | solution.py:373
  30.9 1.2 %copy-start.3 = (bf16[896,896]{1,0:T(8,128)(2,1)}, bf16[896,896]{1,0:T(8,128)(2,1)S(1)}, u32[]{:S(2)}) copy-start(bf16[896,896]{1,0:T(8,128)(2,1)S(1)} %get-tuple-element.109.wq) | copy-start | bytes 4816900
  32.1 1.2 %copy-start.5 = (bf16[896,896]{1,0:T(8,128)(2,1)}, bf16[896,896]{1,0:T(8,128)(2,1)S(1)}, u32[]{:S(2)}) copy-start(bf16[896,896]{1,0:T(8,128)(2,1)S(1)} %get-tuple-element.106.wo) | copy-start | bytes 4816900
  33.3 18.9 %copy-start.9 = (bf16[256,512]{1,0:T(8,128)(2,1)S(1)}, bf16[256,512]{1,0:T(8,128)(2,1)}, u32[]{:S(2)}) copy-start(bf16[256,512]{1,0:T(8,128)(2,1)} %rest_4_.1) | copy-start | bytes 786436
  33.3 18.9 %copy-start.12 = (bf16[2,128,896]{2,1,0:T(8,128)(2,1)S(1)}, bf16[2,128,896]{2,1,0:T(8,128)(2,1)}, u32[]{:S(2)}) copy-start(bf16[2,128,896]{2,1,0:T(8,128)(2,1)} %get-tuple-element.56.e00) | copy-start | bytes 1376260
  33.3 18.9 %copy-start.19 = (s32[4,2]{0,1:T(2,128)S(1)}, s32[4,2]{0,1:T(2,128)}, u32[]{:S(2)}) copy-start(s32[4,2]{0,1:T(2,128)} %param.22) | copy-start | bytes 100
  36.7 11.7 %collective-permute-start.4 = (bf16[2,128,896]{2,1,0:T(8,128)(2,1)}, bf16[2,128,896]{2,1,0:T(8,128)(2,1)S(1)}, u32[]{:S(2)}, u32[]{:S(2)}) collective-permute-start(bf16[2,128,896]{2,1,0:T(8,128)(2,1)} %collective-permute-done.3.e11), channel_id=1, source_target_pairs={{0,6},{2,0},{4,2},{6,4},{1,7},{3,1},{5,3},{7,5},{8,14},{10,8},{12,... | collective-permute-start | bytes 1376264 | tf_op jit(solution)/shard_map/ppermute | solution.py:394
  40.4 22.8 %collective-permute-start.7 = (bf16[4,2,256,128]{3,2,1,0:T(8,128)(2,1)S(1)}, bf16[4,2,256,128]{3,2,1,0:T(8,128)(2,1)S(1)}, u32[]{:S(2)}, u32[]{:S(2)}) collective-permute-start(bf16[4,2,256,128]{3,2,1,0:T(8,128)(2,1)S(1)} %slice.12.kv0), channel_id=1, source_target_pairs={{0,8},{8,0},{1,9},{9,1},{2,10},{10,2},{3,11},{11,3},{4,12},{12,4},... | collective-permute-start | bytes 1572872 | tf_op jit(solution)/shard_map/ppermute | solution.py:389
  40.4 22.8 %collective-permute-start.8 = (bf16[4,2,256,128]{3,2,1,0:T(8,128)(2,1)S(1)}, bf16[4,2,256,128]{3,2,1,0:T(8,128)(2,1)S(1)}, u32[]{:S(2)}, u32[]{:S(2)}) collective-permute-start(bf16[4,2,256,128]{3,2,1,0:T(8,128)(2,1)S(1)} %slice.12.kv0), channel_id=1, source_target_pairs={{0,16},{16,0},{1,17},{17,1},{2,18},{18,2},{3,19},{19,3},{4,20},{20... | collective-permute-start | bytes 1572872 | tf_op jit(solution)/shard_map/ppermute | solution.py:390
  41.1 24.5 %collective-permute-start.9 = (bf16[4,2,256,128]{3,2,1,0:T(8,128)(2,1)S(1)}, bf16[4,2,256,128]{3,2,1,0:T(8,128)(2,1)S(1)}, u32[]{:S(2)}, u32[]{:S(2)}) collective-permute-start(bf16[4,2,256,128]{3,2,1,0:T(8,128)(2,1)S(1)} %slice.12.kv0), channel_id=1, source_target_pairs={{0,24},{8,16},{16,8},{24,0},{1,25},{9,17},{17,9},{25,1},{2,26},{10... | collective-permute-start | bytes 1572872 | tf_op jit(solution)/shard_map/ppermute | solution.py:391
  42.3 1.0 copy-start.8
  43.2 1.2 %copy-start.10 = (bf16[896,512]{1,0:T(8,128)(2,1)S(1)}, bf16[896,512]{1,0:T(8,128)(2,1)}, u32[]{:S(2)}) copy-start(bf16[896,512]{1,0:T(8,128)(2,1)} %kw) | copy-start | bytes 2752516
  44.4 1.2 %copy-start.11 = (bf16[896,512]{1,0:T(8,128)(2,1)S(1)}, bf16[896,512]{1,0:T(8,128)(2,1)}, u32[]{:S(2)}) copy-start(bf16[896,512]{1,0:T(8,128)(2,1)} %vw) | copy-start | bytes 2752516
  61.1 11.3 %collective-permute-start.6 = (bf16[2,128,896]{2,1,0:T(8,128)(2,1)S(1)}, bf16[2,128,896]{2,1,0:T(8,128)(2,1)S(1)}, u32[]{:S(2)}, u32[]{:S(2)}) collective-permute-start(bf16[2,128,896]{2,1,0:T(8,128)(2,1)S(1)} %get-tuple-element.78), channel_id=1, source_target_pairs={{0,6},{2,0},{4,2},{6,4},{1,7},{3,1},{5,3},{7,5},{8,14},{10,8},{12,... | collective-permute-start | bytes 1376264 | tf_op jit(solution)/shard_map/ppermute | solution.py:439
  61.2 24.4 %collective-permute-start.11 = (bf16[4,128,896]{2,1,0:T(8,128)(2,1)S(1)}, bf16[4,128,896]{2,1,0:T(8,128)(2,1)S(1)}, u32[]{:S(2)}, u32[]{:S(2)}) collective-permute-start(bf16[4,128,896]{2,1,0:T(8,128)(2,1)S(1)} %get-tuple-element.90), channel_id=1, source_target_pairs={{0,2},{2,4},{4,6},{6,0},{1,3},{3,5},{5,7},{7,1},{8,10},{10,12},{12... | collective-permute-start | bytes 2752520 | tf_op jit(solution)/shard_map/ppermute | solution.py:440
  72.5 13.0 %collective-permute-start.10 = (bf16[2,128,896]{2,1,0:T(8,128)(2,1)S(1)}, bf16[2,128,896]{2,1,0:T(8,128)(2,1)S(1)}, u32[]{:S(2)}, u32[]{:S(2)}) collective-permute-start(bf16[2,128,896]{2,1,0:T(8,128)(2,1)S(1)} %add_convert_fusion.2), channel_id=1, source_target_pairs={{0,6},{2,0},{4,2},{6,4},{1,7},{3,1},{5,3},{7,5},{8,14},{10,8},{12,... | collective-permute-start | bytes 1376264 | tf_op jit(solution)/shard_map/ppermute | solution.py:454
  72.7 6.4 %collective-permute-start.12 = (bf16[256,128]{1,0:T(8,128)(2,1)S(1)}, bf16[256,128]{1,0:T(8,128)(2,1)S(1)}, u32[]{:S(2)}, u32[]{:S(2)}) collective-permute-start(bf16[256,128]{1,0:T(8,128)(2,1)S(1)} %get-tuple-element.93), channel_id=1, source_target_pairs={{0,96},{32,0},{64,32},{96,64},{1,97},{33,1},{65,33},{97,65},{2,98}... | collective-permute-start | bytes 196616 | tf_op jit(solution)/shard_map/ppermute | solution.py:453
  75.7 6.4 %collective-permute-start.13 = (bf16[256,128]{1,0:T(8,128)(2,1)S(1)}, bf16[256,128]{1,0:T(8,128)(2,1)S(1)}, u32[]{:S(2)}, u32[]{:S(2)}) collective-permute-start(bf16[256,128]{1,0:T(8,128)(2,1)S(1)} %get-tuple-element.94), channel_id=1, source_target_pairs={{0,64},{32,96},{64,0},{96,32},{1,65},{33,97},{65,1},{97,33},{2,66}... | collective-permute-start | bytes 196616 | tf_op jit(solution)/shard_map/ppermute | solution.py:453
  76.5 6.3 %collective-permute-start.14 = (bf16[256,128]{1,0:T(8,128)(2,1)S(1)}, bf16[256,128]{1,0:T(8,128)(2,1)S(1)}, u32[]{:S(2)}, u32[]{:S(2)}) collective-permute-start(bf16[256,128]{1,0:T(8,128)(2,1)S(1)} %get-tuple-element.95), channel_id=1, source_target_pairs={{0,32},{32,64},{64,96},{96,0},{1,33},{33,65},{65,97},{97,1},{2,34}... | collective-permute-start | bytes 196616 | tf_op jit(solution)/shard_map/ppermute | solution.py:453
  85.6 14.1 %copy-start.4 = (bf16[896,896]{1,0:T(8,128)(2,1)S(1)}, bf16[896,896]{1,0:T(8,128)(2,1)}, u32[]{:S(2)}) copy-start(bf16[896,896]{1,0:T(8,128)(2,1)} %copy-done.3) | copy-start | bytes 4816900
  85.6 14.1 %copy-start.6 = (bf16[896,896]{1,0:T(8,128)(2,1)S(1)}, bf16[896,896]{1,0:T(8,128)(2,1)}, u32[]{:S(2)}) copy-start(bf16[896,896]{1,0:T(8,128)(2,1)} %copy-done.5) | copy-start | bytes 4816900
  85.6 14.1 %copy-start.13 = (f32[2,256,128]{2,1,0:T(8,128)S(1)}, f32[2,256,128]{2,1,0:T(8,128)}, u32[]{:S(2)}) copy-start(f32[2,256,128]{2,1,0:T(8,128)} %get-tuple-element.57.wt) | copy-start | bytes 786436
  85.6 14.1 %copy-start.17 = (bf16[2,64,896]{2,1,0:T(8,128)(2,1)S(1)}, bf16[2,64,896]{2,1,0:T(8,128)(2,1)}, u32[]{:S(2)}) copy-start(bf16[2,64,896]{2,1,0:T(8,128)(2,1)} %get-tuple-element.108.ek) | copy-start | bytes 688132
  85.6 14.1 %copy-start.18 = (bf16[2,64,896]{2,1,0:T(8,128)(2,1)S(1)}, bf16[2,64,896]{2,1,0:T(8,128)(2,1)}, u32[]{:S(2)}) copy-start(bf16[2,64,896]{2,1,0:T(8,128)(2,1)} %get-tuple-element.107.ev) | copy-start | bytes 688132
  85.9 13.4 %collective-permute-start.15 = (bf16[2,128,896]{2,1,0:T(8,128)(2,1)S(1)}, bf16[2,128,896]{2,1,0:T(8,128)(2,1)S(1)}, u32[]{:S(2)}, u32[]{:S(2)}) collective-permute-start(bf16[2,128,896]{2,1,0:T(8,128)(2,1)S(1)} %get-tuple-element.111), channel_id=1, source_target_pairs={{0,2},{2,4},{4,6},{6,0},{1,3},{3,5},{5,7},{7,1},{8,10},{10,12},{12... | collective-permute-start | bytes 1376264 | tf_op jit(solution)/shard_map/ppermute | solution.py:459
  86.0 13.7 %collective-permute-start.17 = (bf16[2,128,896]{2,1,0:T(8,128)(2,1)S(1)}, bf16[2,128,896]{2,1,0:T(8,128)(2,1)S(1)}, u32[]{:S(2)}, u32[]{:S(2)}) collective-permute-start(bf16[2,128,896]{2,1,0:T(8,128)(2,1)S(1)} %get-tuple-element.110), channel_id=1, source_target_pairs={{0,1},{1,0},{2,3},{3,2},{4,5},{5,4},{6,7},{7,6},{8,9},{9,8},{10,11... | collective-permute-start | bytes 1376264 | tf_op jit(solution)/shard_map/ppermute | solution.py:458
  86.9 12.8 %collective-permute-start.16 = (bf16[2,128,896]{2,1,0:T(8,128)(2,1)S(1)}, bf16[2,128,896]{2,1,0:T(8,128)(2,1)S(1)}, u32[]{:S(2)}, u32[]{:S(2)}) collective-permute-start(bf16[2,128,896]{2,1,0:T(8,128)(2,1)S(1)} %get-tuple-element.103), channel_id=1, source_target_pairs={{0,6},{2,0},{4,2},{6,4},{1,7},{3,1},{5,3},{7,5},{8,14},{10,8},{12,... | collective-permute-start | bytes 1376264 | tf_op jit(solution)/shard_map/ppermute | solution.py:460

commit v3 on v2

--- a/solution.py
+++ b/solution.py
@@ -196,6 +196,12 @@
     out[...] = (d + mm(jnp.concatenate(back, axis=0), wq[...])).reshape(slots, rows, width)
 
 
+def join_kernel(first, second, out):
+    slots = first.shape[0]
+    out[:slots] = first[...]
+    out[slots:] = second[...]
+
+
 def turn_kernel(wq, wo, wq_t, wo_t):
     wq_t[...] = wq[...].T
     wo_t[...] = wo[...].T
@@ -370,7 +376,13 @@
 
     e01, e30, e10, packed = after((e01, e30, e10, packed))
     e11 = lax.ppermute(e01, "z", shift(NX, -1))
-    up = lax.ppermute(jnp.concatenate([e01, e30]), "z", shift(NX, 1))
+    joined = call(
+        join_kernel,
+        out_shape=struct((2 * slots, nl, ew), BF16),
+        in_specs=[vmem()] * 2,
+        out_specs=vmem(),
+    )(e01, e30)
+    up = lax.ppermute(joined, "z", shift(NX, 1))
 
 
     weights = after((enc_q, enc_o, e01))[:2]

time: 103 us -> 103 us (level)
  Pallas kernels: 27.8 us -> 30 us
  other arithmetic: 2.56 us -> 0.39 us
    concatenate x1 -> x0, other arithmetic: 2.17 us -> none  [local(): up = lax.ppermute(jnp.concatenate([e01, e30]), 'z', shift(NX, 1))]
    pallas_call x0 -> x1, Pallas kernels: none -> 2.15 us  [local(): call(join_kernel, out_shape=struct((2 * slots, nl, ew), BF16), in_specs=[...]
  transfers between devices with their start and end apart: 19 -> 19, of which waited for: 12 -> 12; matrix products, arithmetic and copies ran while one was open for 3% -> 1% of each run, Pallas kernels for 18% -> 20%
where the time goes in v3:
time: 103 us
  waiting for transfers between devices  32.1 us (31%)
  starting transfers between devices  31.5 us (31%)
  Pallas kernels  30 us (29%)
  local copies, waits for them, and re-layouts  7.73 us (8%)
    pallas_call x1, Pallas kernels, local(): call(cross_kernel, out_shape=[struct((rows, width), F32)] + [struct((k *...  8.97 us
    ppermute x1, waiting for transfers between devices, local(): up0 = lax.ppermute(near0, 'z', shift(NX, 1))  8.43 us
    pallas_call x1, Pallas kernels, local(): call(attend_kernel, out_shape=[struct((rows, HSIZE), BF16)] * NX, in_spec...  6.82 us
    unnamed x40, local copies, waits for them, and re-layouts  6.58 us
    pallas_call x1, Pallas kernels, local(): call(encode_kernel, mib=56, out_shape=[struct((slots, nl, ew), BF16), str...  6.25 us
    ppermute x3, waiting for transfers between devices, local(): lax.ppermute(outs[d], 'x', shift(NX, -d))  5.44 us
    ppermute x3, starting transfers between devices, local(): lax.ppermute(outs[d], 'x', shift(NX, -d))  4.68 us
    all_to_all x1, starting transfers between devices, local(): pieces = lax.all_to_all(packed, 'x', 0, 0)  4.54 us
  transfers between devices with their start and end apart: 19, of which 12 were waited for; matrix products, arithmetic and copies ran while one was open for 1% of the time, Pallas kernels for 20%

profile of v3, /device:TPU:0, one launch (start us, length us, event | category | flops | bytes accessed | tf_op | source)
XLA Modules:
  0.0 102.6 jit_solution(4427087934098323233)
XLA Ops:
  0.6 0.0 copy-start.14
  0.6 0.0 copy-start.15
  0.7 0.0 copy-start.16
  0.7 6.2 %shard_map.149 = (bf16[2,128,896]{2,1,0:T(8,128)(2,1)}, f32[2,256,128]{2,1,0:T(8,128)}, bf16[2,64,896]{2,1,0:T(8,128)(2,1)}, bf16[2,64,896]{2,1,0:T(8,128)(2,1)}) custom-call(s32[2,4]{1,0:T(2,128)} %bitcast.1, bf16[2,128,896]{2,1,0:T(8,128)(2,1)} %nb_h.1, bf16[256,896]{1,0:T(8,128)(2,1)} %ctx_h.1, bf16[896,896]{1,0:T(8,128)(2,1)} %wq, ...), custom_call_target="tpu_custom_call" | custom-call | tf_op jit(solution)/shard_map/pallas_call | solution.py:348
  6.9 3.4 %collective-permute-start = (bf16[2,128,896]{2,1,0:T(8,128)(2,1)}, bf16[2,128,896]{2,1,0:T(8,128)(2,1)}, u32[]{:S(2)}, u32[]{:S(2)}) collective-permute-start(bf16[2,128,896]{2,1,0:T(8,128)(2,1)} %get-tuple-element.56.e00), channel_id=1, source_target_pairs={{0,1},{1,0},{2,3},{3,2},{4,5},{5,4},{6,7},{7,6},{8,9},{9,8},{10,11... | collective-permute-start | bytes 1376264 | tf_op jit(solution)/shard_map/ppermute | solution.py:364
  10.3 1.9 %collective-permute-start.1 = (bf16[2,128,896]{2,1,0:T(8,128)(2,1)}, bf16[2,128,896]{2,1,0:T(8,128)(2,1)}, u32[]{:S(2)}, u32[]{:S(2)}) collective-permute-start(bf16[2,128,896]{2,1,0:T(8,128)(2,1)} %get-tuple-element.56.e00), channel_id=1, source_target_pairs={{0,2},{2,4},{4,6},{6,0},{1,3},{3,5},{5,7},{7,1},{8,10},{10,12},{12... | collective-permute-start | bytes 1376264 | tf_op jit(solution)/shard_map/ppermute | solution.py:365
  12.2 2.1 %collective-permute-start.2 = (bf16[2,128,896]{2,1,0:T(8,128)(2,1)}, bf16[2,128,896]{2,1,0:T(8,128)(2,1)}, u32[]{:S(2)}, u32[]{:S(2)}) collective-permute-start(bf16[2,128,896]{2,1,0:T(8,128)(2,1)} %get-tuple-element.56.e00), channel_id=1, source_target_pairs={{0,6},{2,0},{4,2},{6,4},{1,7},{3,1},{5,3},{7,5},{8,14},{10,8},{12,... | collective-permute-start | bytes 1376264 | tf_op jit(solution)/shard_map/ppermute | solution.py:366
  14.3 0.0 copy-done.14
  14.3 0.0 copy-done.16
  14.3 0.1 shard_map.150
  14.5 0.9 copy-done.2
  15.4 4.5 %all-to-all-start = ((bf16[4,3,256,128]{3,2,1,0:T(8,128)(2,1)}), bf16[4,3,256,128]{3,2,1,0:T(8,128)(2,1)}, u32[]{:S(2)}, u32[]{:S(2)}) async-start(bf16[4,3,256,128]{3,2,1,0:T(8,128)(2,1)} %copy-done.2), calls=%async_computation | async-start | bytes 1572864 | tf_op jit(solution)/shard_map/all_to_all | solution.py:375
  19.9 1.2 %collective-permute-done.first.e01 = bf16[2,128,896]{2,1,0:T(8,128)(2,1)} collective-permute-done((bf16[2,128,896]{2,1,0:T(8,128)(2,1)}, bf16[2,128,896]{2,1,0:T(8,128)(2,1)}, u32[]{:S(2)}, u32[]{:S(2)}) %collective-permute-start) | collective-permute-done | bytes 458784 | tf_op jit(solution)/shard_map/ppermute | solution.py:364
  21.1 3.8 %collective-permute-done.1.second.e30 = bf16[2,128,896]{2,1,0:T(8,128)(2,1)} collective-permute-done((bf16[2,128,896]{2,1,0:T(8,128)(2,1)}, bf16[2,128,896]{2,1,0:T(8,128)(2,1)}, u32[]{:S(2)}, u32[]{:S(2)}) %collective-permute-start.1) | collective-permute-done | bytes 458784 | tf_op jit(solution)/shard_map/ppermute | solution.py:365
  24.9 0.0 collective-permute-done.2.e10
  24.9 2.9 %collective-permute-start.3 = (bf16[2,128,896]{2,1,0:T(8,128)(2,1)}, bf16[2,128,896]{2,1,0:T(8,128)(2,1)}, u32[]{:S(2)}, u32[]{:S(2)}) collective-permute-start(bf16[2,128,896]{2,1,0:T(8,128)(2,1)} %collective-permute-done.first.e01), channel_id=1, source_target_pairs={{0,6},{2,0},{4,2},{6,4},{1,7},{3,1},{5,3},{7,5},{8,14},{10,8},{12,... | collective-permute-start | bytes 1376264 | tf_op jit(solution)/shard_map/ppermute | solution.py:378
  27.8 2.1 %shard_map.152 = bf16[4,128,896]{2,1,0:T(8,128)(2,1)} custom-call(bf16[2,128,896]{2,1,0:T(8,128)(2,1)} %collective-permute-done.first.e01, bf16[2,128,896]{2,1,0:T(8,128)(2,1)} %collective-permute-done.1.second.e30), custom_call_target="tpu_custom_call" | custom-call | tf_op jit(solution)/shard_map/pallas_call | solution.py:379
  30.0 0.0 collective-permute-start.5
  30.0 0.0 copy-done
  30.0 0.9 shard_map.151
  30.9 1.2 %copy-done.3 = bf16[896,896]{1,0:T(8,128)(2,1)} copy-done((bf16[896,896]{1,0:T(8,128)(2,1)}, bf16[896,896]{1,0:T(8,128)(2,1)S(1)}, u32[]{:S(2)}) %copy-start.3) | copy-done | bytes 1605656
  32.0 1.2 %copy-done.5 = bf16[896,896]{1,0:T(8,128)(2,1)} copy-done((bf16[896,896]{1,0:T(8,128)(2,1)}, bf16[896,896]{1,0:T(8,128)(2,1)S(1)}, u32[]{:S(2)}) %copy-start.5) | copy-done | bytes 1605656
  33.2 0.0 all-to-all-done.pieces
  33.2 1.1 %slice.12.kv0 = bf16[4,2,256,128]{3,2,1,0:T(8,128)(2,1)S(1)} slice(bf16[4,3,256,128]{3,2,1,0:T(8,128)(2,1)} %all-to-all-done.pieces), slice={[0:4], [1:3], [0:256], [0:128]} | slice | bytes 1048576 | tf_op jit(solution)/shard_map/slice | solution.py:396
  34.4 2.3 %collective-permute-done.3.e11 = bf16[2,128,896]{2,1,0:T(8,128)(2,1)} collective-permute-done((bf16[2,128,896]{2,1,0:T(8,128)(2,1)}, bf16[2,128,896]{2,1,0:T(8,128)(2,1)}, u32[]{:S(2)}, u32[]{:S(2)}) %collective-permute-start.3) | collective-permute-done | bytes 458784 | tf_op jit(solution)/shard_map/ppermute | solution.py:378
  36.7 3.7 %collective-permute-start.4 = (bf16[2,128,896]{2,1,0:T(8,128)(2,1)}, bf16[2,128,896]{2,1,0:T(8,128)(2,1)S(1)}, u32[]{:S(2)}, u32[]{:S(2)}) collective-permute-start(bf16[2,128,896]{2,1,0:T(8,128)(2,1)} %collective-permute-done.3.e11), channel_id=1, source_target_pairs={{0,6},{2,0},{4,2},{6,4},{1,7},{3,1},{5,3},{7,5},{8,14},{10,8},{12,... | collective-permute-start | bytes 1376264 | tf_op jit(solution)/shard_map/ppermute | solution.py:406
  40.4 0.0 collective-permute-start.7
  40.4 0.7 collective-permute-start.8
  41.1 1.2 %collective-permute-start.9 = (bf16[4,2,256,128]{3,2,1,0:T(8,128)(2,1)S(1)}, bf16[4,2,256,128]{3,2,1,0:T(8,128)(2,1)S(1)}, u32[]{:S(2)}, u32[]{:S(2)}) collective-permute-start(bf16[4,2,256,128]{3,2,1,0:T(8,128)(2,1)S(1)} %slice.12.kv0), channel_id=1, source_target_pairs={{0,24},{8,16},{16,8},{24,0},{1,25},{9,17},{17,9},{25,1},{2,26},{10... | collective-permute-start | bytes 1572872 | tf_op jit(solution)/shard_map/ppermute | solution.py:403
  42.3 0.9 copy-done.8
  43.2 1.2 %copy-done.10 = bf16[896,512]{1,0:T(8,128)(2,1)S(1)} copy-done((bf16[896,512]{1,0:T(8,128)(2,1)S(1)}, bf16[896,512]{1,0:T(8,128)(2,1)}, u32[]{:S(2)}) %copy-start.10) | copy-done | bytes 917528
  44.4 1.2 %copy-done.11 = bf16[896,512]{1,0:T(8,128)(2,1)S(1)} copy-done((bf16[896,512]{1,0:T(8,128)(2,1)S(1)}, bf16[896,512]{1,0:T(8,128)(2,1)}, u32[]{:S(2)}) %copy-start.11) | copy-done | bytes 917528
  45.6 1.1 %shard_map.153 = (bf16[896,1024]{1,0:T(8,128)(2,1)S(1)}, bf16[1024,896]{1,0:T(8,128)(2,1)S(1)}, bf16[4,512,256]{2,1,0:T(8,128)(2,1)S(1)}, bf16[4,512,256]{2,1,0:T(8,128)(2,1)S(1)}) custom-call(bf16[896,512]{1,0:T(8,128)(2,1)S(1)} %copy-done.10, bf16[896,512]{1,0:T(8,128)(2,1)S(1)} %copy-done.11, bf16[256,512]{1,0:T(8,128)(2,1)S(1)} %copy-done.7, ...), custom_call_target="tpu_custom_call" | custom-call | tf_op jit(solution)/shard_map/pallas_call | solution.py:409
  46.7 1.6 %collective-permute-done.4.e21 = bf16[2,128,896]{2,1,0:T(8,128)(2,1)S(1)} collective-permute-done((bf16[2,128,896]{2,1,0:T(8,128)(2,1)}, bf16[2,128,896]{2,1,0:T(8,128)(2,1)S(1)}, u32[]{:S(2)}, u32[]{:S(2)}) %collective-permute-start.4) | collective-permute-done | bytes 458784 | tf_op jit(solution)/shard_map/ppermute | solution.py:406
  48.4 3.7 %collective-permute-done.5.up = bf16[4,128,896]{2,1,0:T(8,128)(2,1)} collective-permute-done((bf16[4,128,896]{2,1,0:T(8,128)(2,1)}, bf16[4,128,896]{2,1,0:T(8,128)(2,1)}, u32[]{:S(2)}, u32[]{:S(2)}) %collective-permute-start.5) | collective-permute-done | bytes 917536 | tf_op jit(solution)/shard_map/ppermute | solution.py:385
  52.1 0.0 copy-done.9
  52.1 0.0 copy-done.19
  52.1 9.0 %shard_map.154 = (f32[256,512]{1,0:T(8,128)S(1)}, bf16[2,128,896]{2,1,0:T(8,128)(2,1)S(1)}, bf16[2,128,896]{2,1,0:T(8,128)(2,1)S(1)}, bf16[2,128,896]{2,1,0:T(8,...) custom-call(s32[2,4]{1,0:T(2,128)S(1)} %bitcast.2, ...), custom_call_target="tpu_custom_call" | custom-call | tf_op jit(solution)/shard_map/pallas_call | solution.py:417
  61.1 0.1 collective-permute-start.6
  61.2 2.0 %collective-permute-start.11 = (bf16[4,128,896]{2,1,0:T(8,128)(2,1)S(1)}, bf16[4,128,896]{2,1,0:T(8,128)(2,1)S(1)}, u32[]{:S(2)}, u32[]{:S(2)}) collective-permute-start(bf16[4,128,896]{2,1,0:T(8,128)(2,1)S(1)} %get-tuple-element.90), channel_id=1, source_target_pairs={{0,2},{2,4},{4,6},{6,0},{1,3},{3,5},{5,7},{7,1},{8,10},{10,12},{12... | collective-permute-start | bytes 2752520 | tf_op jit(solution)/shard_map/ppermute | solution.py:452
  63.2 0.0 collective-permute-done.7.kv1
  63.2 0.0 collective-permute-done.8.kv2
  63.2 2.4 %collective-permute-done.9.kv3 = bf16[4,2,256,128]{3,2,1,0:T(8,128)(2,1)S(1)} collective-permute-done((bf16[4,2,256,128]{3,2,1,0:T(8,128)(2,1)S(1)}, bf16[4,2,256,128]{3,2,1,0:T(8,128)(2,1)S(1)}, u32[]{:S(2)}, u32[]{:S(2)}) %collective-permute-start.9) | collective-permute-done | bytes 524320 | tf_op jit(solution)/shard_map/ppermute | solution.py:403
  65.6 6.8 %shard_map.155 = (bf16[256,128]{1,0:T(8,128)(2,1)S(1)}, bf16[256,128]{1,0:T(8,128)(2,1)S(1)}, bf16[256,128]{1,0:T(8,128)(2,1)S(1)}, bf16[256,128]{1,0:T(8,128)(2,1)S(1)}) custom-call(bf16[4,3,256,128]{3,2,1,0:T(8,128)(2,1)} %all-to-all-done.pieces, bf16[4,2,256,128]{3,2,1,0:T(8,128)(2,1)S(1)} %slice.12.kv0, ...), custom_call_target="tpu_custom_call" | custom-call | tf_op jit(solution)/shard_map/pallas_call | solution.py:454
  72.4 0.0 collective-permute-done.6
  72.4 0.1 add_convert_fusion.2
  72.5 0.1 collective-permute-start.10
  72.7 3.0 %collective-permute-start.12 = (bf16[256,128]{1,0:T(8,128)(2,1)S(1)}, bf16[256,128]{1,0:T(8,128)(2,1)S(1)}, u32[]{:S(2)}, u32[]{:S(2)}) collective-permute-start(bf16[256,128]{1,0:T(8,128)(2,1)S(1)} %get-tuple-element.93), channel_id=1, source_target_pairs={{0,96},{32,0},{64,32},{96,64},{1,97},{33,1},{65,33},{97,65},{2,98}... | collective-permute-start | bytes 196616 | tf_op jit(solution)/shard_map/ppermute | solution.py:465
  75.7 0.8 collective-permute-start.13
  76.5 0.9 collective-permute-start.14
  77.4 1.8 %collective-permute-done.12.s1 = bf16[256,128]{1,0:T(8,128)(2,1)S(1)} collective-permute-done((bf16[256,128]{1,0:T(8,128)(2,1)S(1)}, bf16[256,128]{1,0:T(8,128)(2,1)S(1)}, u32[]{:S(2)}, u32[]{:S(2)}) %collective-permute-start.12) | collective-permute-done | bytes 65568 | tf_op jit(solution)/shard_map/ppermute | solution.py:465
  79.1 3.0 %collective-permute-done.13.s2 = bf16[256,128]{1,0:T(8,128)(2,1)S(1)} collective-permute-done((bf16[256,128]{1,0:T(8,128)(2,1)S(1)}, bf16[256,128]{1,0:T(8,128)(2,1)S(1)}, u32[]{:S(2)}, u32[]{:S(2)}) %collective-permute-start.13) | collective-permute-done | bytes 65568 | tf_op jit(solution)/shard_map/ppermute | solution.py:465
  82.1 0.7 collective-permute-done.14.s3
  82.8 2.7 %collective-permute-done.10 = bf16[2,128,896]{2,1,0:T(8,128)(2,1)S(1)} collective-permute-done((bf16[2,128,896]{2,1,0:T(8,128)(2,1)S(1)}, bf16[2,128,896]{2,1,0:T(8,128)(2,1)S(1)}, u32[]{:S(2)}, u32[]{:S(2)}) %collective-permute-start.10) | collective-permute-done | bytes 458784 | tf_op jit(solution)/shard_map/ppermute | solution.py:466
  85.5 0.0 collective-permute-done.11
  85.6 0.3 add_convert_fusion
  85.9 0.1 collective-permute-start.15
  86.0 1.0 collective-permute-start.17
  86.9 3.1 %collective-permute-start.16 = (bf16[2,128,896]{2,1,0:T(8,128)(2,1)S(1)}, bf16[2,128,896]{2,1,0:T(8,128)(2,1)S(1)}, u32[]{:S(2)}, u32[]{:S(2)}) collective-permute-start(bf16[2,128,896]{2,1,0:T(8,128)(2,1)S(1)} %get-tuple-element.103), channel_id=1, source_target_pairs={{0,6},{2,0},{4,2},{6,4},{1,7},{3,1},{5,3},{7,5},{8,14},{10,8},{12,... | collective-permute-start | bytes 1376264 | tf_op jit(solution)/shard_map/ppermute | solution.py:472
  90.1 0.8 shard_map.156
  90.9 8.4 %collective-permute-done.15.d1 = bf16[2,128,896]{2,1,0:T(8,128)(2,1)S(1)} collective-permute-done((bf16[2,128,896]{2,1,0:T(8,128)(2,1)S(1)}, bf16[2,128,896]{2,1,0:T(8,128)(2,1)S(1)}, u32[]{:S(2)}, u32[]{:S(2)}) %collective-permute-start.15) | collective-permute-done | bytes 458784 | tf_op jit(solution)/shard_map/ppermute | solution.py:471
  99.3 0.4 collective-permute-done.17.d3
  99.7 0.0 collective-permute-done.16.d2
  99.7 2.8 %shard_map.157 = f32[2,128,896]{2,1,0:T(8,128)} custom-call(bf16[2,128,896]{2,1,0:T(8,128)(2,1)S(1)} %get-tuple-element.100.d0, bf16[2,128,896]{2,1,0:T(8,128)(2,1)S(1)} %collective-permute-done.15.d1, bf16[2,128,896]{2,1,0:T(8,128)(2,1)S(1)} %collective-permute-done.16.d2, bf16[2,128,896]{2,1,0:T(8,128)(2,1)S(1)} %collective-permute-done.17.d3, ...), custom_call_target="tpu_custom_call" | custom-call | tf_op jit(solution)/shard_map/pallas_call | solution.py:474
  (26 shorter events, 0.0 us)
Async XLA Ops:
  0.6 13.7 %copy-start.14 = (bf16[256,512]{1,0:T(8,128)(2,1)S(1)}, bf16[256,512]{1,0:T(8,128)(2,1)}, u32[]{:S(2)}) copy-start(bf16[256,512]{1,0:T(8,128)(2,1)} %q_ref) | copy-start | bytes 786436
  0.6 13.7 %copy-start.15 = (bf16[256,512]{1,0:T(8,128)(2,1)S(1)}, bf16[256,512]{1,0:T(8,128)(2,1)}, u32[]{:S(2)}) copy-start(bf16[256,512]{1,0:T(8,128)(2,1)} %k_ref) | copy-start | bytes 786436
  0.7 13.7 %copy-start.16 = (bf16[256,512]{1,0:T(8,128)(2,1)S(1)}, bf16[256,512]{1,0:T(8,128)(2,1)}, u32[]{:S(2)}) copy-start(bf16[256,512]{1,0:T(8,128)(2,1)} %v_ref) | copy-start | bytes 786436
  6.9 14.2 %collective-permute-start = (bf16[2,128,896]{2,1,0:T(8,128)(2,1)}, bf16[2,128,896]{2,1,0:T(8,128)(2,1)}, u32[]{:S(2)}, u32[]{:S(2)}) collective-permute-start(bf16[2,128,896]{2,1,0:T(8,128)(2,1)} %get-tuple-element.56.e00), channel_id=1, source_target_pairs={{0,1},{1,0},{2,3},{3,2},{4,5},{5,4},{6,7},{7,6},{8,9},{9,8},{10,11... | collective-permute-start | bytes 1376264 | tf_op jit(solution)/shard_map/ppermute | solution.py:364
  10.3 14.6 %collective-permute-start.1 = (bf16[2,128,896]{2,1,0:T(8,128)(2,1)}, bf16[2,128,896]{2,1,0:T(8,128)(2,1)}, u32[]{:S(2)}, u32[]{:S(2)}) collective-permute-start(bf16[2,128,896]{2,1,0:T(8,128)(2,1)} %get-tuple-element.56.e00), channel_id=1, source_target_pairs={{0,2},{2,4},{4,6},{6,0},{1,3},{3,5},{5,7},{7,1},{8,10},{10,12},{12... | collective-permute-start | bytes 1376264 | tf_op jit(solution)/shard_map/ppermute | solution.py:365
  12.2 12.7 %collective-permute-start.2 = (bf16[2,128,896]{2,1,0:T(8,128)(2,1)}, bf16[2,128,896]{2,1,0:T(8,128)(2,1)}, u32[]{:S(2)}, u32[]{:S(2)}) collective-permute-start(bf16[2,128,896]{2,1,0:T(8,128)(2,1)} %get-tuple-element.56.e00), channel_id=1, source_target_pairs={{0,6},{2,0},{4,2},{6,4},{1,7},{3,1},{5,3},{7,5},{8,14},{10,8},{12,... | collective-permute-start | bytes 1376264 | tf_op jit(solution)/shard_map/ppermute | solution.py:366
  14.5 0.9 copy-start.2
  15.4 14.6 %copy-start = (bf16[896,896]{1,0:T(8,128)(2,1)S(1)}, bf16[896,896]{1,0:T(8,128)(2,1)}, u32[]{:S(2)}) copy-start(bf16[896,896]{1,0:T(8,128)(2,1)} %wq) | copy-start | bytes 4816900
  15.4 14.6 %copy-start.1 = (bf16[896,896]{1,0:T(8,128)(2,1)S(1)}, bf16[896,896]{1,0:T(8,128)(2,1)}, u32[]{:S(2)}) copy-start(bf16[896,896]{1,0:T(8,128)(2,1)} %wo) | copy-start | bytes 4816900
  15.4 17.9 %all-to-all-start = ((bf16[4,3,256,128]{3,2,1,0:T(8,128)(2,1)}), bf16[4,3,256,128]{3,2,1,0:T(8,128)(2,1)}, u32[]{:S(2)}, u32[]{:S(2)}) async-start(bf16[4,3,256,128]{3,2,1,0:T(8,128)(2,1)} %copy-done.2), calls=%async_computation | async-start | bytes 1572864 | tf_op jit(solution)/shard_map/all_to_all | solution.py:375
  24.9 11.8 %collective-permute-start.3 = (bf16[2,128,896]{2,1,0:T(8,128)(2,1)}, bf16[2,128,896]{2,1,0:T(8,128)(2,1)}, u32[]{:S(2)}, u32[]{:S(2)}) collective-permute-start(bf16[2,128,896]{2,1,0:T(8,128)(2,1)} %collective-permute-done.first.e01), channel_id=1, source_target_pairs={{0,6},{2,0},{4,2},{6,4},{1,7},{3,1},{5,3},{7,5},{8,14},{10,8},{12,... | collective-permute-start | bytes 1376264 | tf_op jit(solution)/shard_map/ppermute | solution.py:378
  30.0 12.3 %copy-start.7 = (bf16[256,512]{1,0:T(8,128)(2,1)S(1)}, bf16[256,512]{1,0:T(8,128)(2,1)}, u32[]{:S(2)}) copy-start(bf16[256,512]{1,0:T(8,128)(2,1)} %rest_3_.1) | copy-start | bytes 786436
  30.0 22.1 %collective-permute-start.5 = (bf16[4,128,896]{2,1,0:T(8,128)(2,1)}, bf16[4,128,896]{2,1,0:T(8,128)(2,1)}, u32[]{:S(2)}, u32[]{:S(2)}) collective-permute-start(bf16[4,128,896]{2,1,0:T(8,128)(2,1)} %shard_map.152), channel_id=1, source_target_pairs={{0,2},{2,4},{4,6},{6,0},{1,3},{3,5},{5,7},{7,1},{8,10},{10,12},{12... | collective-permute-start | bytes 2752520 | tf_op jit(solution)/shard_map/ppermute | solution.py:385
  30.9 1.2 %copy-start.3 = (bf16[896,896]{1,0:T(8,128)(2,1)}, bf16[896,896]{1,0:T(8,128)(2,1)S(1)}, u32[]{:S(2)}) copy-start(bf16[896,896]{1,0:T(8,128)(2,1)S(1)} %get-tuple-element.109.wq) | copy-start | bytes 4816900
  32.0 1.2 %copy-start.5 = (bf16[896,896]{1,0:T(8,128)(2,1)}, bf16[896,896]{1,0:T(8,128)(2,1)S(1)}, u32[]{:S(2)}) copy-start(bf16[896,896]{1,0:T(8,128)(2,1)S(1)} %get-tuple-element.106.wo) | copy-start | bytes 4816900
  33.2 18.9 %copy-start.9 = (bf16[256,512]{1,0:T(8,128)(2,1)S(1)}, bf16[256,512]{1,0:T(8,128)(2,1)}, u32[]{:S(2)}) copy-start(bf16[256,512]{1,0:T(8,128)(2,1)} %rest_4_.1) | copy-start | bytes 786436
  33.2 18.9 %copy-start.12 = (bf16[2,128,896]{2,1,0:T(8,128)(2,1)S(1)}, bf16[2,128,896]{2,1,0:T(8,128)(2,1)}, u32[]{:S(2)}) copy-start(bf16[2,128,896]{2,1,0:T(8,128)(2,1)} %get-tuple-element.56.e00) | copy-start | bytes 1376260
  33.2 18.9 %copy-start.19 = (s32[4,2]{0,1:T(2,128)S(1)}, s32[4,2]{0,1:T(2,128)}, u32[]{:S(2)}) copy-start(s32[4,2]{0,1:T(2,128)} %param.22) | copy-start | bytes 100
  36.7 11.7 %collective-permute-start.4 = (bf16[2,128,896]{2,1,0:T(8,128)(2,1)}, bf16[2,128,896]{2,1,0:T(8,128)(2,1)S(1)}, u32[]{:S(2)}, u32[]{:S(2)}) collective-permute-start(bf16[2,128,896]{2,1,0:T(8,128)(2,1)} %collective-permute-done.3.e11), channel_id=1, source_target_pairs={{0,6},{2,0},{4,2},{6,4},{1,7},{3,1},{5,3},{7,5},{8,14},{10,8},{12,... | collective-permute-start | bytes 1376264 | tf_op jit(solution)/shard_map/ppermute | solution.py:406
  40.4 22.8 %collective-permute-start.7 = (bf16[4,2,256,128]{3,2,1,0:T(8,128)(2,1)S(1)}, bf16[4,2,256,128]{3,2,1,0:T(8,128)(2,1)S(1)}, u32[]{:S(2)}, u32[]{:S(2)}) collective-permute-start(bf16[4,2,256,128]{3,2,1,0:T(8,128)(2,1)S(1)} %slice.12.kv0), channel_id=1, source_target_pairs={{0,8},{8,0},{1,9},{9,1},{2,10},{10,2},{3,11},{11,3},{4,12},{12,4},... | collective-permute-start | bytes 1572872 | tf_op jit(solution)/shard_map/ppermute | solution.py:401
  40.4 22.8 %collective-permute-start.8 = (bf16[4,2,256,128]{3,2,1,0:T(8,128)(2,1)S(1)}, bf16[4,2,256,128]{3,2,1,0:T(8,128)(2,1)S(1)}, u32[]{:S(2)}, u32[]{:S(2)}) collective-permute-start(bf16[4,2,256,128]{3,2,1,0:T(8,128)(2,1)S(1)} %slice.12.kv0), channel_id=1, source_target_pairs={{0,16},{16,0},{1,17},{17,1},{2,18},{18,2},{3,19},{19,3},{4,20},{20... | collective-permute-start | bytes 1572872 | tf_op jit(solution)/shard_map/ppermute | solution.py:402
  41.1 24.5 %collective-permute-start.9 = (bf16[4,2,256,128]{3,2,1,0:T(8,128)(2,1)S(1)}, bf16[4,2,256,128]{3,2,1,0:T(8,128)(2,1)S(1)}, u32[]{:S(2)}, u32[]{:S(2)}) collective-permute-start(bf16[4,2,256,128]{3,2,1,0:T(8,128)(2,1)S(1)} %slice.12.kv0), channel_id=1, source_target_pairs={{0,24},{8,16},{16,8},{24,0},{1,25},{9,17},{17,9},{25,1},{2,26},{10... | collective-permute-start | bytes 1572872 | tf_op jit(solution)/shard_map/ppermute | solution.py:403
  42.3 1.0 copy-start.8
  43.2 1.2 %copy-start.10 = (bf16[896,512]{1,0:T(8,128)(2,1)S(1)}, bf16[896,512]{1,0:T(8,128)(2,1)}, u32[]{:S(2)}) copy-start(bf16[896,512]{1,0:T(8,128)(2,1)} %kw) | copy-start | bytes 2752516
  44.4 1.2 %copy-start.11 = (bf16[896,512]{1,0:T(8,128)(2,1)S(1)}, bf16[896,512]{1,0:T(8,128)(2,1)}, u32[]{:S(2)}) copy-start(bf16[896,512]{1,0:T(8,128)(2,1)} %vw) | copy-start | bytes 2752516
  61.1 11.3 %collective-permute-start.6 = (bf16[2,128,896]{2,1,0:T(8,128)(2,1)S(1)}, bf16[2,128,896]{2,1,0:T(8,128)(2,1)S(1)}, u32[]{:S(2)}, u32[]{:S(2)}) collective-permute-start(bf16[2,128,896]{2,1,0:T(8,128)(2,1)S(1)} %get-tuple-element.78), channel_id=1, source_target_pairs={{0,6},{2,0},{4,2},{6,4},{1,7},{3,1},{5,3},{7,5},{8,14},{10,8},{12,... | collective-permute-start | bytes 1376264 | tf_op jit(solution)/shard_map/ppermute | solution.py:451
  61.2 24.4 %collective-permute-start.11 = (bf16[4,128,896]{2,1,0:T(8,128)(2,1)S(1)}, bf16[4,128,896]{2,1,0:T(8,128)(2,1)S(1)}, u32[]{:S(2)}, u32[]{:S(2)}) collective-permute-start(bf16[4,128,896]{2,1,0:T(8,128)(2,1)S(1)} %get-tuple-element.90), channel_id=1, source_target_pairs={{0,2},{2,4},{4,6},{6,0},{1,3},{3,5},{5,7},{7,1},{8,10},{10,12},{12... | collective-permute-start | bytes 2752520 | tf_op jit(solution)/shard_map/ppermute | solution.py:452
  72.5 13.0 %collective-permute-start.10 = (bf16[2,128,896]{2,1,0:T(8,128)(2,1)S(1)}, bf16[2,128,896]{2,1,0:T(8,128)(2,1)S(1)}, u32[]{:S(2)}, u32[]{:S(2)}) collective-permute-start(bf16[2,128,896]{2,1,0:T(8,128)(2,1)S(1)} %add_convert_fusion.2), channel_id=1, source_target_pairs={{0,6},{2,0},{4,2},{6,4},{1,7},{3,1},{5,3},{7,5},{8,14},{10,8},{12,... | collective-permute-start | bytes 1376264 | tf_op jit(solution)/shard_map/ppermute | solution.py:466
  72.7 6.5 %collective-permute-start.12 = (bf16[256,128]{1,0:T(8,128)(2,1)S(1)}, bf16[256,128]{1,0:T(8,128)(2,1)S(1)}, u32[]{:S(2)}, u32[]{:S(2)}) collective-permute-start(bf16[256,128]{1,0:T(8,128)(2,1)S(1)} %get-tuple-element.93), channel_id=1, source_target_pairs={{0,96},{32,0},{64,32},{96,64},{1,97},{33,1},{65,33},{97,65},{2,98}... | collective-permute-start | bytes 196616 | tf_op jit(solution)/shard_map/ppermute | solution.py:465
  75.7 6.4 %collective-permute-start.13 = (bf16[256,128]{1,0:T(8,128)(2,1)S(1)}, bf16[256,128]{1,0:T(8,128)(2,1)S(1)}, u32[]{:S(2)}, u32[]{:S(2)}) collective-permute-start(bf16[256,128]{1,0:T(8,128)(2,1)S(1)} %get-tuple-element.94), channel_id=1, source_target_pairs={{0,64},{32,96},{64,0},{96,32},{1,65},{33,97},{65,1},{97,33},{2,66}... | collective-permute-start | bytes 196616 | tf_op jit(solution)/shard_map/ppermute | solution.py:465
  76.5 6.3 %collective-permute-start.14 = (bf16[256,128]{1,0:T(8,128)(2,1)S(1)}, bf16[256,128]{1,0:T(8,128)(2,1)S(1)}, u32[]{:S(2)}, u32[]{:S(2)}) collective-permute-start(bf16[256,128]{1,0:T(8,128)(2,1)S(1)} %get-tuple-element.95), channel_id=1, source_target_pairs={{0,32},{32,64},{64,96},{96,0},{1,33},{33,65},{65,97},{97,1},{2,34}... | collective-permute-start | bytes 196616 | tf_op jit(solution)/shard_map/ppermute | solution.py:465
  85.6 14.1 %copy-start.4 = (bf16[896,896]{1,0:T(8,128)(2,1)S(1)}, bf16[896,896]{1,0:T(8,128)(2,1)}, u32[]{:S(2)}) copy-start(bf16[896,896]{1,0:T(8,128)(2,1)} %copy-done.3) | copy-start | bytes 4816900
  85.6 14.1 %copy-start.6 = (bf16[896,896]{1,0:T(8,128)(2,1)S(1)}, bf16[896,896]{1,0:T(8,128)(2,1)}, u32[]{:S(2)}) copy-start(bf16[896,896]{1,0:T(8,128)(2,1)} %copy-done.5) | copy-start | bytes 4816900
  85.6 14.1 %copy-start.13 = (f32[2,256,128]{2,1,0:T(8,128)S(1)}, f32[2,256,128]{2,1,0:T(8,128)}, u32[]{:S(2)}) copy-start(f32[2,256,128]{2,1,0:T(8,128)} %get-tuple-element.57.wt) | copy-start | bytes 786436
  85.6 14.1 %copy-start.17 = (bf16[2,64,896]{2,1,0:T(8,128)(2,1)S(1)}, bf16[2,64,896]{2,1,0:T(8,128)(2,1)}, u32[]{:S(2)}) copy-start(bf16[2,64,896]{2,1,0:T(8,128)(2,1)} %get-tuple-element.108.ek) | copy-start | bytes 688132
  85.6 14.1 %copy-start.18 = (bf16[2,64,896]{2,1,0:T(8,128)(2,1)S(1)}, bf16[2,64,896]{2,1,0:T(8,128)(2,1)}, u32[]{:S(2)}) copy-start(bf16[2,64,896]{2,1,0:T(8,128)(2,1)} %get-tuple-element.107.ev) | copy-start | bytes 688132
  85.9 13.4 %collective-permute-start.15 = (bf16[2,128,896]{2,1,0:T(8,128)(2,1)S(1)}, bf16[2,128,896]{2,1,0:T(8,128)(2,1)S(1)}, u32[]{:S(2)}, u32[]{:S(2)}) collective-permute-start(bf16[2,128,896]{2,1,0:T(8,128)(2,1)S(1)} %get-tuple-element.111), channel_id=1, source_target_pairs={{0,2},{2,4},{4,6},{6,0},{1,3},{3,5},{5,7},{7,1},{8,10},{10,12},{12... | collective-permute-start | bytes 1376264 | tf_op jit(solution)/shard_map/ppermute | solution.py:471
  86.0 13.7 %collective-permute-start.17 = (bf16[2,128,896]{2,1,0:T(8,128)(2,1)S(1)}, bf16[2,128,896]{2,1,0:T(8,128)(2,1)S(1)}, u32[]{:S(2)}, u32[]{:S(2)}) collective-permute-start(bf16[2,128,896]{2,1,0:T(8,128)(2,1)S(1)} %get-tuple-element.110), channel_id=1, source_target_pairs={{0,1},{1,0},{2,3},{3,2},{4,5},{5,4},{6,7},{7,6},{8,9},{9,8},{10,11... | collective-permute-start | bytes 1376264 | tf_op jit(solution)/shard_map/ppermute | solution.py:470
  86.9 12.8 %collective-permute-start.16 = (bf16[2,128,896]{2,1,0:T(8,128)(2,1)S(1)}, bf16[2,128,896]{2,1,0:T(8,128)(2,1)S(1)}, u32[]{:S(2)}, u32[]{:S(2)}) collective-permute-start(bf16[2,128,896]{2,1,0:T(8,128)(2,1)S(1)} %get-tuple-element.103), channel_id=1, source_target_pairs={{0,6},{2,0},{4,2},{6,4},{1,7},{3,1},{5,3},{7,5},{8,14},{10,8},{12,... | collective-permute-start | bytes 1376264 | tf_op jit(solution)/shard_map/ppermute | solution.py:472
